TPU v7x, 1024 devices: a whole 4x4x32 slice. The times are simulated.
1024 devices in a mesh: dp: 8 (over y_hi, x), ctx: 128 (over y_lo, z, core).
Axes of the slice: x: 4, y: 4 (y_hi: 2, y_lo: 2; y = y_hi * 2 + y_lo), z: 32, core: 2. Of those that a mesh axis runs over, the one named last changes fastest.
Arguments:
- queries: bfloat16 [131072, 2048], P(('dp', 'ctx')), parts along dimension 0, may hold values from -12 to 12
- keys: bfloat16 [131072, 2048], P(('dp', 'ctx')), parts along dimension 0, may hold values from -12 to 12
- values: bfloat16 [131072, 2048], P(('dp', 'ctx')), parts along dimension 0, may hold values from -6 to 6
- dout: bfloat16 [131072, 2048], P(('dp', 'ctx')), parts along dimension 0, may hold values from -48 to 48
- global_block: int32 [8], P('dp'), parts along dimension 0, may hold values from 0 to 127
Outputs:
- key_grad: bfloat16 [131072, 2048], P(('dp', 'ctx')), parts along dimension 0
- value_grad: bfloat16 [131072, 2048], P(('dp', 'ctx')), parts along dimension 0
There are 8 independent parts, one for each index of `dp`. A program takes and returns all parts, laid end to end along the dimension named above; each array names one. Nothing has to cross between parts.
All inputs are finite; a program needn't handle non-finite values.
Results may differ from a plain program's by a relative error of at most 0.0054.
Values may be sent and summed in bfloat16 or wider, within the bound.
No kernel may reach another device: no remote copies, remote signals or barrier semaphores. Data moves between devices by JAX's collectives and lax.ppermute only.
A program may use at most 64 MiB of HBM per device.

v0:
```python
import jax
import jax.numpy as jnp
from jax import lax
from jax.sharding import PartitionSpec as P

HEADS = 16
HEAD_DIM = 128
LEVELS = 2
GLOBALS = 1


def swapped(value, axis, apart):
    mask = 2**apart
    pairs = [(source, source ^ mask) for source in range(lax.axis_size(axis))]
    return lax.ppermute(value, axis, pairs)


def from_root(value, axis, source):
    kept = jnp.where(lax.axis_index(axis) == source, value, 0).astype(value.dtype)
    return lax.psum(kept, axis)


def key_terms(logit_grad, prob_low, query_rows, dout_rows, inv_root):
    key_part = (
        jnp.einsum("hqk,qhd->khd", logit_grad, query_rows, preferred_element_type=jnp.float32)
        * inv_root
    )
    value_part = jnp.einsum("hqk,qhd->khd", prob_low, dout_rows, preferred_element_type=jnp.float32)
    return (key_part, value_part)


def body(queries, keys, values, dout, global_block):
    row_count = queries.shape[0]
    head_shape = (row_count, HEADS, HEAD_DIM)
    inv_root = HEAD_DIM ** (-0.5)
    own_index = lax.axis_index("ctx")
    q_own = queries.reshape(head_shape)
    d_own = dout.reshape(head_shape)
    key_sets = [keys]
    value_sets = [values]
    for section_bit in range(LEVELS):
        got_key, got_value = swapped((keys, values), "ctx", section_bit)
        key_sets.append(got_key)
        value_sets.append(got_value)
    slot = 0
    got_key = from_root(keys, "ctx", global_block[slot])
    got_value = from_root(values, "ctx", global_block[slot])
    key_sets.append(got_key)
    value_sets.append(got_value)
    key_rows = jnp.concatenate(key_sets, axis=0).reshape(-1, HEADS, HEAD_DIM)
    value_rows = jnp.concatenate(value_sets, axis=0).reshape(-1, HEADS, HEAD_DIM)
    logits = (
        jnp.einsum("qhd,khd->hqk", q_own, key_rows, preferred_element_type=jnp.float32) * inv_root
    )
    row_top = jnp.max(logits, axis=2)
    log_total = row_top + jnp.log(jnp.sum(jnp.exp(logits - row_top[:, :, None]), axis=2))
    prob_grad = jnp.einsum("qhd,khd->hqk", d_own, value_rows, preferred_element_type=jnp.float32)
    row_delta = jnp.sum(jnp.exp(logits - log_total[:, :, None]) * prob_grad, axis=2)
    logit_grad = (
        jnp.exp(logits - log_total[:, :, None]) * (prob_grad - row_delta[:, :, None])
    ).astype(jnp.bfloat16)
    prob_low = jnp.exp(logits - log_total[:, :, None]).astype(jnp.bfloat16)
    glob_start = (1 + LEVELS) * row_count
    all_key, all_value = key_terms(logit_grad, prob_low, q_own, d_own, inv_root)
    key_part = all_key[:row_count]
    value_part = all_value[:row_count]
    for section_bit in range(LEVELS):
        lower = (1 + section_bit) * row_count
        upper = lower + row_count
        back_key, back_value = swapped(
            (
                all_key[lower:upper].astype(jnp.bfloat16),
                all_value[lower:upper].astype(jnp.bfloat16),
            ),
            "ctx",
            section_bit,
        )
        key_part = key_part + back_key.astype(jnp.float32)
        value_part = value_part + back_value.astype(jnp.float32)
    glob_key = all_key[glob_start:]
    glob_value = all_value[glob_start:]
    glob_key = glob_key.reshape(GLOBALS, row_count, HEADS, HEAD_DIM)
    glob_value = glob_value.reshape(GLOBALS, row_count, HEADS, HEAD_DIM)
    total_key, total_value = lax.psum((glob_key, glob_value), "ctx")
    slot = 0
    chosen = own_index == global_block[slot]
    key_part = key_part + jnp.where(chosen, total_key[slot], jnp.float32(0.0))
    value_part = value_part + jnp.where(chosen, total_value[slot], jnp.float32(0.0))
    key_out = key_part.astype(jnp.bfloat16).reshape(row_count, -1)
    value_out = value_part.astype(jnp.bfloat16).reshape(row_count, -1)
    return (key_out, value_out)


def solution(mesh):
    return jax.shard_map(
        body,
        mesh=mesh,
        in_specs=(
            P(("dp", "ctx"), None),
            P(("dp", "ctx"), None),
            P(("dp", "ctx"), None),
            P(("dp", "ctx"), None),
            P("dp"),
        ),
        out_specs=(P(("dp", "ctx"), None), P(("dp", "ctx"), None)),
        check_vma=False,
    )
```

profile of v0, /device:TPU:1, one launch (start us, length us, event | category | flops | bytes accessed | tf_op | source)
XLA Modules:
  0.0 1734.9 jit_solution(5366883718755296755)
XLA Ops:
  7.2 0.0 all-reduce.7.cloned.1.call-start
  8.0 1.3 copy.18
  9.3 1.3 copy.24
  10.6 0.8 broadcast_select_fusion
  11.4 0.8 broadcast_select_fusion.1
  12.3 0.0 all-reduce.7.cloned.1.call-update
  12.3 0.0 all-reduce.5.cloned.1.call-start
  12.3 4.4 collective-permute-start.1
  16.7 13.6 collective-permute-start
  30.3 3.6 collective-permute-start.3
  34.0 2.2 collective-permute-start.2
  36.2 0.3 copy.43
  36.5 0.0 copy-done.4
  36.5 1.0 copy.44
  37.5 0.0 collective-permute-done.1
  37.5 0.0 collective-permute-done
  37.5 831.5 %all-reduce.7.cloned.1.call-done = (bf16[128,2048]{0,1:T(8,128)(2,1)}, bf16[128,2048]{0,1:T(8,128)(2,1)}) async-done(((bf16[128,2048]{0,1:T(8,128)(2,1)}, bf16[128,2048]{0,1:T(8,128)(2,1)}), (bf16[128,2048]{0,1:T(8,128)(2,1)}, bf16[128,2048]{0,1:T(8,128)(2,1)})) %all-reduce.7.cloned.1.call-update) | async-done | bytes 1048592 | tf_op jit(solution)/shard_map/psum | solution.py:20
  869.0 1.4 pad_maximum_fusion
  870.5 0.0 copy-start.2
  870.5 0.9 bitcast_reduce_fusion
  871.4 0.7 fusion.4
  872.1 0.9 fusion.25
  873.0 0.0 collective-permute-done.3
  873.0 0.0 collective-permute-done.2
  873.0 0.1 copy-done.5
  873.2 2.2 pad_maximum_fusion.1
  875.4 1.3 fusion
  876.7 2.8 fusion.24
  879.5 2.0 copy-done
  881.5 1.1 slice_bitcast_fusion.1
  882.6 1.0 slice_bitcast_fusion
  883.7 0.0 all-reduce.5.cloned.1.call-update
  883.7 1.3 fusion.23
  885.0 4.9 collective-permute-start.4
  889.8 1.9 collective-permute-start.5
  891.8 0.1 fusion.22
  891.9 1.9 collective-permute-start.6
  893.8 3.6 collective-permute-start.7
  897.5 0.0 collective-permute-done.4
  897.5 8.1 collective-permute-done.5
  905.6 0.0 collective-permute-done.6
  905.6 11.6 collective-permute-done.7
  917.2 806.1 %all-reduce.5.cloned.1.call-done = (f32[1,128,16,128]{3,1,2,0:T(8,128)}, f32[1,128,16,128]{3,1,2,0:T(8,128)}) async-done(((f32[1,128,16,128]{3,1,2,0:T(8,128)}, f32[1,128,16,128]{3,1,2,0:T(8,128)}), (f32[1,128,16,128]{3,1,2,0:T(8,128)}, f32[1,128,16,128]{3,1,2,0:T(8,128)})) %all-reduce.5.cloned.1.call-update) | async-done | bytes 2097168 | tf_op jit(solution)/shard_map/psum | solution.py:84
  1723.2 2.2 fusion.16
  1725.5 0.3 copy.34
  1725.7 1.0 copy.36
  1726.8 0.3 copy.30
  1727.0 1.0 copy.35
  (9 shorter events, 0.0 us)
Async XLA Ops:
  7.2 29.0 %copy-start.3 = (bf16[128,2048]{1,0:T(8,128)(2,1)S(1)}, bf16[128,2048]{1,0:T(8,128)(2,1)}, u32[]{:S(2)}) copy-start(bf16[128,2048]{1,0:T(8,128)(2,1)} %param.5) | copy-start | bytes 1572868
  7.2 29.3 %copy-start.4 = (bf16[128,2048]{1,0:T(8,128)(2,1)S(1)}, bf16[128,2048]{1,0:T(8,128)(2,1)}, u32[]{:S(2)}) copy-start(bf16[128,2048]{1,0:T(8,128)(2,1)} %param.8) | copy-start | bytes 1572868
  7.2 861.9 %all-reduce.7.cloned.1.call-start = ((), (), s32[]{:S(2)}) async-start(), calls=%async_computation.1 | async-start | bytes 2097152 | tf_op jit(solution)/shard_map/psum | solution.py:20
  12.3 1711.0 %all-reduce.5.cloned.1.call-start = ((), (), s32[]{:S(2)}) async-start(), calls=%async_computation | async-start | bytes 4194304 | tf_op jit(solution)/shard_map/psum | solution.py:84
  12.3 25.2 %collective-permute-start.1 = (bf16[128,2048]{0,1:T(8,128)(2,1)S(1)}, bf16[128,2048]{0,1:T(8,128)(2,1)S(1)}, u32[]{:S(2)}, u32[]{:S(2)}) collective-permute-start(bf16[128,2048]{0,1:T(8,128)(2,1)S(1)} %copy.18), channel_id=1, source_target_pairs={{0,2},{1,3},{2,0},{3,1},{4,6},{5,7},{6,4},{7,5},{8,10},{9,11},{10,... | collective-permute-start | bytes 1572872 | tf_op jit(solution)/shard_map/ppermute | solution.py:15
  16.7 20.8 %collective-permute-start = (bf16[128,2048]{0,1:T(8,128)(2,1)S(1)}, bf16[128,2048]{0,1:T(8,128)(2,1)}, u32[]{:S(2)}, u32[]{:S(2)}) collective-permute-start(bf16[128,2048]{0,1:T(8,128)(2,1)S(1)} %copy.18), channel_id=1, source_target_pairs={{0,1},{1,0},{2,3},{3,2},{4,5},{5,4},{6,7},{7,6},{8,9},{9,8},{10,11... | collective-permute-start | bytes 1572872 | tf_op jit(solution)/shard_map/ppermute | solution.py:15
  30.3 842.7 %collective-permute-start.3 = (bf16[128,2048]{0,1:T(8,128)(2,1)S(1)}, bf16[128,2048]{0,1:T(8,128)(2,1)}, u32[]{:S(2)}, u32[]{:S(2)}) collective-permute-start(bf16[128,2048]{0,1:T(8,128)(2,1)S(1)} %copy.24), channel_id=1, source_target_pairs={{0,2},{1,3},{2,0},{3,1},{4,6},{5,7},{6,4},{7,5},{8,10},{9,11},{10,... | collective-permute-start | bytes 1572872 | tf_op jit(solution)/shard_map/ppermute | solution.py:15
  34.0 839.0 %collective-permute-start.2 = (bf16[128,2048]{0,1:T(8,128)(2,1)S(1)}, bf16[128,2048]{0,1:T(8,128)(2,1)}, u32[]{:S(2)}, u32[]{:S(2)}) collective-permute-start(bf16[128,2048]{0,1:T(8,128)(2,1)S(1)} %copy.24), channel_id=1, source_target_pairs={{0,1},{1,0},{2,3},{3,2},{4,5},{5,4},{6,7},{7,6},{8,9},{9,8},{10,11... | collective-permute-start | bytes 1572872 | tf_op jit(solution)/shard_map/ppermute | solution.py:15
  870.5 1.6 copy-start.2
  872.1 1.0 copy-start.5
  873.0 9.6 copy-start.1
  879.5 2.0 copy-start
  885.0 12.5 collective-permute-start.4
  889.8 15.7 collective-permute-start.5
  891.9 13.7 collective-permute-start.6
  893.8 23.3 %collective-permute-start.7 = (bf16[128,16,128]{2,0,1:T(8,128)(2,1)S(1)}, bf16[128,16,128]{2,0,1:T(8,128)(2,1)S(1)}, u32[]{:S(2)}, u32[]{:S(2)}) collective-permute-start(bf16[128,16,128]{2,0,1:T(8,128)(2,1)S(1)} %get-tuple-element.9), channel_id=1, source_target_pairs={{0,2},{1,3},{2,0},{3,1},{4,6},{5,7},{6,4},{7,5},{8,10},{9,11},{10,... | collective-permute-start | bytes 1572872 | tf_op jit(solution)/shard_map/ppermute | solution.py:15
Sparse Core Ops, SparseCore 0:
  12.4 856.5 all-reduce.6
  883.8 839.4 all-reduce.4
where the time goes:
time: 1740 us; the launch traced here: 1730 us
  waiting for transfers between devices  1660 us (95%)
  starting transfers between devices  36.3 us (2%)
    psum x1, waiting for transfers between devices, from_root(): return lax.psum(kept, axis)  832 us
    psum x1, waiting for transfers between devices, body(): total_key, total_value = lax.psum((glob_key, glob_value), 'ctx')  806 us
    ppermute x8, starting transfers between devices, swapped(): return lax.ppermute(value, axis, pairs)  36.2 us
  transfers between devices with their start and end apart: 10, of which 4 were waited for; matrix products, arithmetic and copies ran while one was open for 0% of the time, Pallas kernels for 0%

commit v1 on v0

v1 whole, which is shorter than its diff:
```python
import jax
import jax.numpy as jnp
from jax import lax
from jax.experimental import pallas as pl
from jax.experimental.pallas import tpu as pltpu
from jax.sharding import PartitionSpec as P

HEADS = 16
HEAD_DIM = 128
BLOCK = 128
LEVELS = 2
WIDTH = HEADS * HEAD_DIM
HEADS_PER_STEP = 4
NEAR = (1, 2, 3, 6)
FAR = (4, 5)
NEAR_COUNT = 1 << len(NEAR)
CHUNK = BLOCK // NEAR_COUNT


def swapped(value, mask):
    pairs = [(source, source ^ mask) for source in range(lax.axis_size("ctx"))]
    return lax.ppermute(value, "ctx", pairs)


def groups(bits):
    spread = [
        sum(((k >> i) & 1) << bit for i, bit in enumerate(bits)) for k in range(1 << len(bits))
    ]
    mask = spread[-1]
    return [
        [base | part for part in spread]
        for base in range(lax.axis_size("ctx"))
        if not base & mask
    ]


def picked(index, bits):
    return sum(((index >> bit) & 1) << i for i, bit in enumerate(bits))


def near_exchange(value):
    return lax.all_to_all(value, "ctx", 0, 0, axis_index_groups=groups(NEAR))


def far_gather(value):
    return lax.all_gather(value, "ctx", axis_index_groups=groups(FAR))


def added(parts):
    terms = [parts[i].astype(jnp.float32) for i in range(parts.shape[0])]
    while len(terms) > 1:
        terms = [a + b for a, b in zip(terms[::2], terms[1::2])]
    return terms[0].astype(jnp.bfloat16)


def near_gather(value):
    copies = jnp.broadcast_to(value[None], (NEAR_COUNT,) + value.shape)
    return near_exchange(copies).reshape(BLOCK, WIDTH)


def attention_kernel(
    core_ref, q_ref, d_ref, k0, k1, k2, ka, v0, v1, v2, va,
    own_k, own_v, b1_k, b1_v, b2_k, b2_v, g_k, g_v,
):
    inv_root = HEAD_DIM ** (-0.5)
    first = core_ref[0] == 0
    last = (((1,), (1,)), ((), ()))
    for h in range(HEADS_PER_STEP):
        cols = pl.ds(h * HEAD_DIM, HEAD_DIM)
        q = q_ref[:, cols]
        d = d_ref[:, cols]
        mine, got = ka[:, cols], va[:, cols]
        key_glob = jnp.where(first, mine, got)
        value_glob = jnp.where(first, got, mine)
        keys = [k0[:, cols], k1[:, cols], k2[:, cols], key_glob]
        values = [v0[:, cols], v1[:, cols], v2[:, cols], value_glob]
        logits = [
            lax.dot_general(k, q, last, preferred_element_type=jnp.float32) * inv_root
            for k in keys
        ]
        top = jnp.max(
            jnp.maximum(jnp.maximum(logits[0], logits[1]), jnp.maximum(logits[2], logits[3])),
            axis=0, keepdims=True,
        )
        exps = [jnp.exp(x - top) for x in logits]
        total = jnp.sum((exps[0] + exps[1]) + (exps[2] + exps[3]), axis=0, keepdims=True)
        scale = 1.0 / total
        probs = [e * scale for e in exps]
        grads = [
            lax.dot_general(v, d, last, preferred_element_type=jnp.float32) for v in values
        ]
        prods = [p * g for p, g in zip(probs, grads)]
        delta = jnp.sum((prods[0] + prods[1]) + (prods[2] + prods[3]), axis=0, keepdims=True)
        outs = ((own_k, own_v), (b1_k, b1_v), (b2_k, b2_v), (g_k, g_v))
        for p, g, (out_k, out_v) in zip(probs, grads, outs):
            low = (p * (g - delta)).astype(jnp.bfloat16)
            key_term = jnp.dot(low, q, preferred_element_type=jnp.float32) * inv_root
            value_term = jnp.dot(
                p.astype(jnp.bfloat16), d, preferred_element_type=jnp.float32
            )
            out_k[:, cols] = key_term.astype(out_k.dtype)
            out_v[:, cols] = value_term.astype(out_v.dtype)


def attention(core, *arrays):
    block = pl.BlockSpec((BLOCK, HEADS_PER_STEP * HEAD_DIM), lambda i: (0, i))
    low = jax.ShapeDtypeStruct((BLOCK, WIDTH), jnp.bfloat16)
    full = jax.ShapeDtypeStruct((BLOCK, WIDTH), jnp.float32)
    return pl.pallas_call(
        attention_kernel,
        grid=(HEADS // HEADS_PER_STEP,),
        in_specs=[pl.BlockSpec(memory_space=pltpu.SMEM)] + [block] * len(arrays),
        out_specs=[block] * 8,
        out_shape=[full, full, low, low, low, low, low, low],
        cost_estimate=pl.CostEstimate(
            flops=2 * 4 * HEADS * BLOCK * 4 * BLOCK * HEAD_DIM,
            bytes_accessed=24 * BLOCK * WIDTH * 2,
            transcendentals=HEADS * BLOCK * 4 * BLOCK,
        ),
        compiler_params=pltpu.CompilerParams(vmem_limit_bytes=32 * 1024 * 1024),
    )(core, *arrays)


def body(queries, keys, values, dout, global_block):
    me = lax.axis_index("ctx")
    root = global_block[0]
    first_core = (me & 1) == 0

    share = jnp.where(first_core, keys, values)
    share_got = swapped(jnp.where(first_core, values, keys), 1)
    rest_got = swapped(share, 1)
    key_1 = jnp.where(first_core, share_got, rest_got)
    value_1 = jnp.where(first_core, rest_got, share_got)
    key_2 = swapped(keys, 2)
    value_2 = swapped(values, 2)

    share = jnp.where(((root ^ me) & 1) == 0, share, share_got)
    chunks = near_exchange(share.reshape(NEAR_COUNT, CHUNK, WIDTH))
    chunk = lax.dynamic_index_in_dim(chunks, picked(root, NEAR), 0, keepdims=False)
    chunk = lax.dynamic_index_in_dim(far_gather(chunk), picked(root, FAR), 0, keepdims=False)
    glob_mine = near_gather(chunk)
    glob_got = swapped(glob_mine, 1)

    core = (me & 1).astype(jnp.int32).reshape(1)
    own_k, own_v, b1_k, b1_v, b2_k, b2_v, g_k, g_v = attention(
        core, queries, dout, keys, key_1, key_2, glob_mine, values, value_1, value_2, glob_got
    )

    part = jnp.where(first_core, g_k, g_v).astype(jnp.float32)
    part = part + swapped(jnp.where(first_core, g_v, g_k), 1).astype(jnp.float32)
    parts = near_exchange(part.astype(jnp.bfloat16).reshape(NEAR_COUNT, CHUNK, WIDTH))
    part = added(far_gather(added(parts)))
    total_mine = near_gather(part)
    total_got = swapped(total_mine, 1)
    total_k = jnp.where(first_core, total_mine, total_got)
    total_v = jnp.where(first_core, total_got, total_mine)

    back_1k, back_1v = swapped((b1_k, b1_v), 1)
    back_2k, back_2v = swapped((b2_k, b2_v), 2)
    chosen = me == root

    def final(own, back_1, back_2, total):
        out = own + back_1.astype(jnp.float32) + back_2.astype(jnp.float32)
        out = out + jnp.where(chosen, total.astype(jnp.float32), jnp.float32(0.0))
        return out.astype(jnp.bfloat16)

    return final(own_k, back_1k, back_2k, total_k), final(own_v, back_1v, back_2v, total_v)


def solution(mesh):
    rows = P(("dp", "ctx"), None)
    return jax.shard_map(
        body,
        mesh=mesh,
        in_specs=(rows, rows, rows, rows, P("dp")),
        out_specs=(rows, rows),
        check_vma=False,
    )
```

time: 1740 us -> 269 us (0.15)
  the two profiles are of different devices: /device:TPU:1 before, /device:TPU:66 now
where the time goes in v1:
time: 269 us; the launch traced here: 268 us
  blocking collectives  98.5 us (37%)
  waiting for transfers between devices  92.4 us (34%)
  starting transfers between devices  52.9 us (20%)
  Pallas kernels  8.38 us (3%)
  other arithmetic  7.23 us (3%)
  local copies, waits for them, and re-layouts  6.69 us (2%)
    all_gather x2, blocking collectives, far_gather(): return lax.all_gather(value, 'ctx', axis_index_groups=groups(FAR))  65 us
    all_to_all x3, waiting for transfers between devices, near_exchange(): return lax.all_to_all(value, 'ctx', 0, 0, axis_index_groups=groups(NEAR))  56.9 us
    ppermute x11, waiting for transfers between devices, swapped(): return lax.ppermute(value, 'ctx', pairs)  35.5 us
    all_to_all x1, blocking collectives, near_exchange(): return lax.all_to_all(value, 'ctx', 0, 0, axis_index_groups=groups(NEAR))  33.5 us
    all_to_all x3, starting transfers between devices, near_exchange(): return lax.all_to_all(value, 'ctx', 0, 0, axis_index_groups=groups(NEAR))  27.5 us
    ppermute x11, starting transfers between devices, swapped(): return lax.ppermute(value, 'ctx', pairs)  25.4 us
    pallas_call x1, Pallas kernels, attention(): pl.pallas_call(attention_kernel, grid=(HEADS // HEADS_PER_STEP,), in_spec...  8.38 us
  transfers between devices with their start and end apart: 14, of which 9 were waited for; matrix products, arithmetic and copies ran while one was open for 0% of the time, Pallas kernels for 0%

profile of v1, /device:TPU:66, one launch (start us, length us, event | category | flops | bytes accessed | tf_op | source)
XLA Modules:
  0.0 267.6 jit_solution(15052663253225152114)
XLA Ops:
  0.7 1.2 broadcast_select_fusion.4
  1.9 1.9 collective-permute-start
  4.4 1.2 collective-permute-done
  5.7 1.1 select_bitcast_fusion
  6.7 13.2 %all-to-all-start = ((bf16[16,8,2048]{2,1,0:T(8,128)(2,1)}), bf16[16,8,2048]{2,1,0:T(8,128)(2,1)S(1)}, u32[]{:S(2)}, u32[]{:S(2)}) async-start(bf16[16,8,2048]{2,1,0:T(8,128)(2,1)} %get-tuple-element.18), calls=%async_computation | async-start | bytes 1048576 | tf_op jit(solution)/shard_map/all_to_all | solution.py:42
  19.9 25.9 %all-to-all-done = bf16[16,8,2048]{2,1,0:T(8,128)(2,1)S(1)} async-done(((bf16[16,8,2048]{2,1,0:T(8,128)(2,1)}), bf16[16,8,2048]{2,1,0:T(8,128)(2,1)S(1)}, u32[]{:S(2)}, u32[]{:S(2)}) %all-to-all-start) | async-done | bytes 524320 | tf_op jit(solution)/shard_map/all_to_all | solution.py:42
  45.8 37.2 %all_gather.8 = bf16[4,8,2048]{2,1,0:T(8,128)(2,1)S(1)} all-gather(bf16[1,8,2048]{2,1,0:T(8,128)(2,1)S(1)} %constant_dynamic-slice_fusion), channel_id=1, replica_groups={{0,16,32,48},{1,17,33,49},{2,18,34,50},{3,19,35,51},{4,20,36,52},{5,21,..., dimensions={0}, use_global_device_ids=true | all-gather | bytes 163840 | tf_op jit(solution)/shard_map/all_gather | solution.py:46
  82.9 0.8 broadcast_in_dim.22
  83.8 7.0 %all-to-all-start.1 = ((bf16[16,8,2048]{2,1,0:T(8,128)(2,1)}), bf16[16,8,2048]{2,1,0:T(8,128)(2,1)S(1)}, u32[]{:S(2)}, u32[]{:S(2)}) async-start(bf16[16,8,2048]{2,1,0:T(8,128)(2,1)} %broadcast_in_dim.22), calls=%async_computation.1 | async-start | bytes 1048576 | tf_op jit(solution)/shard_map/all_to_all | solution.py:42
  90.8 1.9 collective-permute-start.1
  92.7 3.4 %collective-permute-start.2 = (bf16[128,2048]{1,0:T(8,128)(2,1)S(1)}, bf16[128,2048]{1,0:T(8,128)(2,1)S(1)}, u32[]{:S(2)}, u32[]{:S(2)}) collective-permute-start(bf16[128,2048]{1,0:T(8,128)(2,1)S(1)} %copy-done), channel_id=1, source_target_pairs={{0,2},{1,3},{2,0},{3,1},{4,6},{5,7},{6,4},{7,5},{8,10},{9,11},{10,... | collective-permute-start | bytes 1572872 | tf_op jit(solution)/shard_map/ppermute | solution.py:22
  96.1 2.5 collective-permute-start.3
  98.6 16.6 %all-to-all-done.1 = bf16[16,8,2048]{2,1,0:T(8,128)(2,1)S(1)} async-done(((bf16[16,8,2048]{2,1,0:T(8,128)(2,1)}), bf16[16,8,2048]{2,1,0:T(8,128)(2,1)S(1)}, u32[]{:S(2)}, u32[]{:S(2)}) %all-to-all-start.1) | async-done | bytes 524320 | tf_op jit(solution)/shard_map/all_to_all | solution.py:42
  115.1 2.0 collective-permute-start.4
  117.2 0.0 collective-permute-done.1
  117.2 1.1 broadcast_select_fusion.1
  118.3 5.2 %collective-permute-done.2.k2 = bf16[128,2048]{1,0:T(8,128)(2,1)S(1)} collective-permute-done((bf16[128,2048]{1,0:T(8,128)(2,1)S(1)}, bf16[128,2048]{1,0:T(8,128)(2,1)S(1)}, u32[]{:S(2)}, u32[]{:S(2)}) %collective-permute-start.2) | collective-permute-done | bytes 524320 | tf_op jit(solution)/shard_map/ppermute | solution.py:22
  123.6 10.3 %collective-permute-done.3.v2 = bf16[128,2048]{1,0:T(8,128)(2,1)S(1)} collective-permute-done((bf16[128,2048]{1,0:T(8,128)(2,1)S(1)}, bf16[128,2048]{1,0:T(8,128)(2,1)S(1)}, u32[]{:S(2)}, u32[]{:S(2)}) %collective-permute-start.3) | collective-permute-done | bytes 524320 | tf_op jit(solution)/shard_map/ppermute | solution.py:22
  133.9 0.8 copy-done.6
  134.7 0.0 collective-permute-done.4.va
  134.7 1.0 copy-done.7
  135.8 8.4 %shard_map.68 = (f32[128,2048]{1,0:T(8,128)S(1)}, f32[128,2048]{1,0:T(8,128)S(1)}, bf16[128,2048]{1,0:T(8,128)(2,1)S(1)}, bf16[128,2048]{1,0:T(8,128)(2,1)S(1)},...) custom-call(s32[1]{0:T(128)} %bitcast.core_ref, ...), custom_call_target="tpu_custom_call" | custom-call | flops 1073741824 | bytes 12582912 | tf_op jit(solution)/shard_map/pallas_call | solution.py:109
  144.1 0.0 copy-start.10
  144.2 0.8 copy-done.10
  144.9 0.8 copy-done.12
  145.7 0.8 copy-done.13
  146.5 0.1 broadcast_select_fusion
  146.6 0.7 copy-done.8
  147.3 1.9 collective-permute-start.7
  149.2 1.9 collective-permute-done.7
  151.1 0.2 fusion
  151.4 33.5 %all_to_all.20 = bf16[16,8,2048]{2,1,0:T(8,128)(2,1)S(1)} all-to-all(bf16[16,8,2048]{2,1,0:T(8,128)(2,1)S(1)} %fusion), channel_id=1, replica_groups={{0,2,4,6,8,10,12,14,64,66,68,70,72,74,76,78},{1,3,5,7,9,11,13,15,65,67,..., dimensions={0} | all-to-all | bytes 1048576 | tf_op jit(solution)/shard_map/all_to_all | solution.py:42
  184.9 0.1 add_convert_fusion.4
  184.9 27.8 %all_gather.9 = bf16[4,8,2048]{2,1,0:T(8,128)(2,1)S(1)} all-gather(bf16[1,8,2048]{2,1,0:T(8,128)(2,1)S(1)} %add_convert_fusion.4), channel_id=1, replica_groups={{0,16,32,48},{1,17,33,49},{2,18,34,50},{3,19,35,51},{4,20,36,52},{5,21,..., dimensions={0}, use_global_device_ids=true | all-gather | bytes 163840 | tf_op jit(solution)/shard_map/all_gather | solution.py:46
  212.8 0.9 broadcast_in_dim.24
  213.7 7.3 %all-to-all-start.3 = ((bf16[16,8,2048]{2,1,0:T(8,128)(2,1)}), bf16[16,8,2048]{2,1,0:T(8,128)(2,1)}, u32[]{:S(2)}, u32[]{:S(2)}) async-start(bf16[16,8,2048]{2,1,0:T(8,128)(2,1)} %broadcast_in_dim.24), calls=%async_computation.3 | async-start | bytes 1048576 | tf_op jit(solution)/shard_map/all_to_all | solution.py:42
  221.0 1.9 collective-permute-start.5
  222.9 3.4 %collective-permute-start.6 = (bf16[128,2048]{1,0:T(8,128)(2,1)}, bf16[128,2048]{1,0:T(8,128)(2,1)}, u32[]{:S(2)}, u32[]{:S(2)}) collective-permute-start(bf16[128,2048]{1,0:T(8,128)(2,1)} %copy-done.12), channel_id=1, source_target_pairs={{0,2},{1,3},{2,0},{3,1},{4,6},{5,7},{6,4},{7,5},{8,10},{9,11},{10,... | collective-permute-start | bytes 1572872 | tf_op jit(solution)/shard_map/ppermute | solution.py:22
  226.3 2.1 collective-permute-start.9
  228.4 2.5 collective-permute-start.10
  230.9 14.5 %all-to-all-done.3 = bf16[16,8,2048]{2,1,0:T(8,128)(2,1)} async-done(((bf16[16,8,2048]{2,1,0:T(8,128)(2,1)}), bf16[16,8,2048]{2,1,0:T(8,128)(2,1)}, u32[]{:S(2)}, u32[]{:S(2)}) %all-to-all-start.3) | async-done | bytes 524320 | tf_op jit(solution)/shard_map/all_to_all | solution.py:42
  245.4 1.9 collective-permute-start.8
  247.3 0.0 collective-permute-done.5
  247.3 6.5 %collective-permute-done.6 = bf16[128,2048]{1,0:T(8,128)(2,1)} collective-permute-done((bf16[128,2048]{1,0:T(8,128)(2,1)}, bf16[128,2048]{1,0:T(8,128)(2,1)}, u32[]{:S(2)}, u32[]{:S(2)}) %collective-permute-start.6) | collective-permute-done | bytes 524320 | tf_op jit(solution)/shard_map/ppermute | solution.py:22
  253.8 0.0 collective-permute-done.9
  253.8 10.3 %collective-permute-done.10 = bf16[128,2048]{1,0:T(8,128)(2,1)} collective-permute-done((bf16[128,2048]{1,0:T(8,128)(2,1)S(1)}, bf16[128,2048]{1,0:T(8,128)(2,1)}, u32[]{:S(2)}, u32[]{:S(2)}) %collective-permute-start.10) | collective-permute-done | bytes 524320 | tf_op jit(solution)/shard_map/ppermute | solution.py:22
  264.1 0.0 collective-permute-done.8
  264.2 3.5 %add_convert_fusion = (bf16[128,2048]{1,0:T(8,128)(2,1)}, bf16[128,2048]{1,0:T(8,128)(2,1)}) fusion(bf16[128,2048]{1,0:T(8,128)(2,1)} %collective-permute-done.10, f32[128,2048]{1,0:T(8,128)S(1)} %copy-done.3, bf16[128,2048]{1,0:T(8,128)(2,1)} %collective-permute-done.9, bf16[128,2048]{1,0:T(8,128)(2,1)} %collective-permute-done.8, pred[]{:T(512)S(6)} %eq.11, ...), kind=kLoop, calls=%fused_computation | loop fusion | flops 4718592 | bytes 6291458 | tf_op jit(solution)/shard_map/convert_element_type | solution.py:165
  (24 shorter events, 0.1 us)
Async XLA Ops:
  0.6 5.0 %copy-start = (bf16[128,2048]{1,0:T(8,128)(2,1)S(1)}, bf16[128,2048]{1,0:T(8,128)(2,1)}, u32[]{:S(2)}) copy-start(bf16[128,2048]{1,0:T(8,128)(2,1)} %k0.1) | copy-start | bytes 1572868
  0.6 5.0 %copy-start.1 = (bf16[128,2048]{1,0:T(8,128)(2,1)S(1)}, bf16[128,2048]{1,0:T(8,128)(2,1)}, u32[]{:S(2)}) copy-start(bf16[128,2048]{1,0:T(8,128)(2,1)} %v0.1) | copy-start | bytes 1572868
  1.9 3.8 %collective-permute-start = (bf16[128,2048]{1,0:T(8,128)(2,1)S(1)}, bf16[128,2048]{1,0:T(8,128)(2,1)S(1)}, u32[]{:S(2)}, u32[]{:S(2)}) collective-permute-start(bf16[128,2048]{1,0:T(8,128)(2,1)S(1)} %broadcast_select_fusion.4), channel_id=1, source_target_pairs={{0,1},{1,0},{2,3},{3,2},{4,5},{5,4},{6,7},{7,6},{8,9},{9,8},{10,11... | collective-permute-start | bytes 1572872 | tf_op jit(solution)/shard_map/ppermute | solution.py:22
  6.7 39.1 %all-to-all-start = ((bf16[16,8,2048]{2,1,0:T(8,128)(2,1)}), bf16[16,8,2048]{2,1,0:T(8,128)(2,1)S(1)}, u32[]{:S(2)}, u32[]{:S(2)}) async-start(bf16[16,8,2048]{2,1,0:T(8,128)(2,1)} %get-tuple-element.18), calls=%async_computation | async-start | bytes 1048576 | tf_op jit(solution)/shard_map/all_to_all | solution.py:42
  83.8 31.4 %all-to-all-start.1 = ((bf16[16,8,2048]{2,1,0:T(8,128)(2,1)}), bf16[16,8,2048]{2,1,0:T(8,128)(2,1)S(1)}, u32[]{:S(2)}, u32[]{:S(2)}) async-start(bf16[16,8,2048]{2,1,0:T(8,128)(2,1)} %broadcast_in_dim.22), calls=%async_computation.1 | async-start | bytes 1048576 | tf_op jit(solution)/shard_map/all_to_all | solution.py:42
  90.8 26.4 %collective-permute-start.1 = (bf16[128,2048]{1,0:T(8,128)(2,1)}, bf16[128,2048]{1,0:T(8,128)(2,1)}, u32[]{:S(2)}, u32[]{:S(2)}) collective-permute-start(bf16[128,2048]{1,0:T(8,128)(2,1)} %get-tuple-element.19), channel_id=1, source_target_pairs={{0,1},{1,0},{2,3},{3,2},{4,5},{5,4},{6,7},{7,6},{8,9},{9,8},{10,11... | collective-permute-start | bytes 1572872 | tf_op jit(solution)/shard_map/ppermute | solution.py:22
  92.7 30.9 %collective-permute-start.2 = (bf16[128,2048]{1,0:T(8,128)(2,1)S(1)}, bf16[128,2048]{1,0:T(8,128)(2,1)S(1)}, u32[]{:S(2)}, u32[]{:S(2)}) collective-permute-start(bf16[128,2048]{1,0:T(8,128)(2,1)S(1)} %copy-done), channel_id=1, source_target_pairs={{0,2},{1,3},{2,0},{3,1},{4,6},{5,7},{6,4},{7,5},{8,10},{9,11},{10,... | collective-permute-start | bytes 1572872 | tf_op jit(solution)/shard_map/ppermute | solution.py:22
  96.1 37.8 %collective-permute-start.3 = (bf16[128,2048]{1,0:T(8,128)(2,1)S(1)}, bf16[128,2048]{1,0:T(8,128)(2,1)S(1)}, u32[]{:S(2)}, u32[]{:S(2)}) collective-permute-start(bf16[128,2048]{1,0:T(8,128)(2,1)S(1)} %copy-done.1), channel_id=1, source_target_pairs={{0,2},{1,3},{2,0},{3,1},{4,6},{5,7},{6,4},{7,5},{8,10},{9,11},{10,... | collective-permute-start | bytes 1572872 | tf_op jit(solution)/shard_map/ppermute | solution.py:22
  115.1 19.6 %copy-start.4 = (bf16[128,2048]{1,0:T(8,128)(2,1)S(1)}, bf16[128,2048]{1,0:T(8,128)(2,1)}, u32[]{:S(2)}) copy-start(bf16[128,2048]{1,0:T(8,128)(2,1)} %q_ref.1) | copy-start | bytes 1572868
  115.1 19.6 %copy-start.5 = (bf16[128,2048]{1,0:T(8,128)(2,1)S(1)}, bf16[128,2048]{1,0:T(8,128)(2,1)}, u32[]{:S(2)}) copy-start(bf16[128,2048]{1,0:T(8,128)(2,1)} %d_ref.1) | copy-start | bytes 1572868
  115.1 19.6 %collective-permute-start.4 = (bf16[128,2048]{1,0:T(8,128)(2,1)S(1)}, bf16[128,2048]{1,0:T(8,128)(2,1)S(1)}, u32[]{:S(2)}, u32[]{:S(2)}) collective-permute-start(bf16[128,2048]{1,0:T(8,128)(2,1)S(1)} %bitcast.22), channel_id=1, source_target_pairs={{0,1},{1,0},{2,3},{3,2},{4,5},{5,4},{6,7},{7,6},{8,9},{9,8},{10,11... | collective-permute-start | bytes 1572872 | tf_op jit(solution)/shard_map/ppermute | solution.py:22
  133.9 0.8 copy-start.6
  134.7 1.0 copy-start.7
  144.1 0.8 copy-start.10
  144.9 0.8 copy-start.12
  145.7 0.8 copy-start.13
  146.5 0.8 copy-start.8
  146.5 4.8 %copy-start.2 = (f32[128,2048]{1,0:T(8,128)}, f32[128,2048]{1,0:T(8,128)S(1)}, u32[]{:S(2)}) copy-start(f32[128,2048]{1,0:T(8,128)S(1)} %get-tuple-element.15) | copy-start | bytes 3145732
  147.3 3.8 %collective-permute-start.7 = (bf16[128,2048]{1,0:T(8,128)(2,1)S(1)}, bf16[128,2048]{1,0:T(8,128)(2,1)S(1)}, u32[]{:S(2)}, u32[]{:S(2)}) collective-permute-start(bf16[128,2048]{1,0:T(8,128)(2,1)S(1)} %broadcast_select_fusion), channel_id=1, source_target_pairs={{0,1},{1,0},{2,3},{3,2},{4,5},{5,4},{6,7},{7,6},{8,9},{9,8},{10,11... | collective-permute-start | bytes 1572872 | tf_op jit(solution)/shard_map/ppermute | solution.py:22
  184.9 41.4 %copy-start.11 = (bf16[128,2048]{1,0:T(8,128)(2,1)S(1)}, bf16[128,2048]{1,0:T(8,128)(2,1)}, u32[]{:S(2)}) copy-start(bf16[128,2048]{1,0:T(8,128)(2,1)} %copy-done.10) | copy-start | bytes 1572868
  184.9 79.2 %copy-start.3 = (f32[128,2048]{1,0:T(8,128)S(1)}, f32[128,2048]{1,0:T(8,128)}, u32[]{:S(2)}) copy-start(f32[128,2048]{1,0:T(8,128)} %copy-done.2) | copy-start | bytes 3145732
  213.7 14.7 %copy-start.9 = (bf16[128,2048]{1,0:T(8,128)(2,1)S(1)}, bf16[128,2048]{1,0:T(8,128)(2,1)}, u32[]{:S(2)}) copy-start(bf16[128,2048]{1,0:T(8,128)(2,1)} %copy-done.8) | copy-start | bytes 1572868
  213.7 31.7 %all-to-all-start.3 = ((bf16[16,8,2048]{2,1,0:T(8,128)(2,1)}), bf16[16,8,2048]{2,1,0:T(8,128)(2,1)}, u32[]{:S(2)}, u32[]{:S(2)}) async-start(bf16[16,8,2048]{2,1,0:T(8,128)(2,1)} %broadcast_in_dim.24), calls=%async_computation.3 | async-start | bytes 1048576 | tf_op jit(solution)/shard_map/all_to_all | solution.py:42
  221.0 26.3 %collective-permute-start.5 = (bf16[128,2048]{1,0:T(8,128)(2,1)}, bf16[128,2048]{1,0:T(8,128)(2,1)}, u32[]{:S(2)}, u32[]{:S(2)}) collective-permute-start(bf16[128,2048]{1,0:T(8,128)(2,1)} %copy-done.13), channel_id=1, source_target_pairs={{0,1},{1,0},{2,3},{3,2},{4,5},{5,4},{6,7},{7,6},{8,9},{9,8},{10,11... | collective-permute-start | bytes 1572872 | tf_op jit(solution)/shard_map/ppermute | solution.py:22
  222.9 30.9 %collective-permute-start.6 = (bf16[128,2048]{1,0:T(8,128)(2,1)}, bf16[128,2048]{1,0:T(8,128)(2,1)}, u32[]{:S(2)}, u32[]{:S(2)}) collective-permute-start(bf16[128,2048]{1,0:T(8,128)(2,1)} %copy-done.12), channel_id=1, source_target_pairs={{0,2},{1,3},{2,0},{3,1},{4,6},{5,7},{6,4},{7,5},{8,10},{9,11},{10,... | collective-permute-start | bytes 1572872 | tf_op jit(solution)/shard_map/ppermute | solution.py:22
  226.3 27.5 %collective-permute-start.9 = (bf16[128,2048]{1,0:T(8,128)(2,1)S(1)}, bf16[128,2048]{1,0:T(8,128)(2,1)}, u32[]{:S(2)}, u32[]{:S(2)}) collective-permute-start(bf16[128,2048]{1,0:T(8,128)(2,1)S(1)} %copy-done.11), channel_id=1, source_target_pairs={{0,1},{1,0},{2,3},{3,2},{4,5},{5,4},{6,7},{7,6},{8,9},{9,8},{10,11... | collective-permute-start | bytes 1572872 | tf_op jit(solution)/shard_map/ppermute | solution.py:22
  228.4 35.7 %collective-permute-start.10 = (bf16[128,2048]{1,0:T(8,128)(2,1)S(1)}, bf16[128,2048]{1,0:T(8,128)(2,1)}, u32[]{:S(2)}, u32[]{:S(2)}) collective-permute-start(bf16[128,2048]{1,0:T(8,128)(2,1)S(1)} %copy-done.9), channel_id=1, source_target_pairs={{0,2},{1,3},{2,0},{3,1},{4,6},{5,7},{6,4},{7,5},{8,10},{9,11},{10,... | collective-permute-start | bytes 1572872 | tf_op jit(solution)/shard_map/ppermute | solution.py:22
  245.4 18.8 %collective-permute-start.8 = (bf16[128,2048]{1,0:T(8,128)(2,1)}, bf16[128,2048]{1,0:T(8,128)(2,1)}, u32[]{:S(2)}, u32[]{:S(2)}) collective-permute-start(bf16[128,2048]{1,0:T(8,128)(2,1)} %bitcast.7), channel_id=1, source_target_pairs={{0,1},{1,0},{2,3},{3,2},{4,5},{5,4},{6,7},{7,6},{8,9},{9,8},{10,11... | collective-permute-start | bytes 1572872 | tf_op jit(solution)/shard_map/ppermute | solution.py:22

commit v2 on v1

v2 whole, which is shorter than its diff:
```python
import jax
import jax.numpy as jnp
from jax import lax
from jax.experimental import pallas as pl
from jax.experimental.pallas import tpu as pltpu
from jax.sharding import PartitionSpec as P

HEADS = 16
HEAD_DIM = 128
BLOCK = 128
LEVELS = 2
WIDTH = HEADS * HEAD_DIM
INV_ROOT = HEAD_DIM ** (-0.5)
STEP_HEADS = 4
STEPS = HEADS // STEP_HEADS
STEP_COLS = STEP_HEADS * HEAD_DIM
STAT_ROWS = 8
TEAM = (0, 1, 2, 6)
QUAD = 4
PAIR_BIT = 3
FAR = (4, 5)
LAST = (((1,), (1,)), ((), ()))


def swapped(value, mask):
    pairs = [(source, source ^ mask) for source in range(lax.axis_size("ctx"))]
    return lax.ppermute(value, "ctx", pairs)


def groups(bits):
    spread = [
        sum(((k >> i) & 1) << bit for i, bit in enumerate(bits)) for k in range(1 << len(bits))
    ]
    mask = spread[-1]
    return [
        [base | part for part in spread]
        for base in range(lax.axis_size("ctx"))
        if not base & mask
    ]


def picked(parts, root, bits):
    index = sum(((root >> bit) & 1) << i for i, bit in enumerate(bits))
    return lax.dynamic_index_in_dim(parts, index, 0, keepdims=False)


def exchange(value, bits):
    return lax.all_to_all(value, "ctx", 0, 0, axis_index_groups=groups(bits))


def far_gather(value):
    return lax.all_gather(value, "ctx", axis_index_groups=groups(FAR))


def added(parts):
    terms = [parts[i].astype(jnp.float32) for i in range(parts.shape[0])]
    while len(terms) > 1:
        terms = [a + b for a, b in zip(terms[::2], terms[1::2])]
    return terms[0].astype(jnp.bfloat16)


def dot_last(a, b):
    return lax.dot_general(a, b, LAST, preferred_element_type=jnp.float32)


def dot(a, b):
    return jnp.dot(a, b, preferred_element_type=jnp.float32)


def sum_rows(value):
    return jnp.sum(value, axis=0, keepdims=True)


def max_rows(value):
    return jnp.max(value, axis=0, keepdims=True)


def cost(dots, exps, size):
    return pl.CostEstimate(
        flops=2 * dots * BLOCK * BLOCK * HEAD_DIM,
        transcendentals=exps * BLOCK * BLOCK,
        bytes_accessed=size * BLOCK * HEAD_DIM * 2,
    )


PARAMS = pltpu.CompilerParams(vmem_limit_bytes=32 * 1024 * 1024)
SCALARS = pl.BlockSpec(memory_space=pltpu.SMEM)
COLS = pl.BlockSpec((BLOCK, QUAD * HEAD_DIM), lambda i: (0, i))
TILES = pl.BlockSpec((QUAD, 2, BLOCK, HEAD_DIM), lambda i: (i, 0, 0, 0))
STATS = pl.BlockSpec((QUAD, STAT_ROWS, BLOCK), lambda i: (i, 0, 0))
WHOLE = pl.BlockSpec(memory_space=pltpu.VMEM)
ROWS_SHAPE = jax.ShapeDtypeStruct((BLOCK, WIDTH), jnp.bfloat16)
TILES_SHAPE = jax.ShapeDtypeStruct((HEADS, 2, BLOCK, HEAD_DIM), jnp.bfloat16)
STATS_SHAPE = jax.ShapeDtypeStruct((HEADS, STAT_ROWS, BLOCK), jnp.float32)
PAIR_SHAPE = jax.ShapeDtypeStruct((2, BLOCK, HEAD_DIM), jnp.float32)


def head(h):
    return pl.ds(h * HEAD_DIM, HEAD_DIM)


def split_kernel(a_ref, b_ref, out_ref):
    for h in range(QUAD):
        out_ref[h, 0] = a_ref[:, head(h)]
        out_ref[h, 1] = b_ref[:, head(h)]


def split_heads(a, b):
    return pl.pallas_call(
        split_kernel,
        grid=(HEADS // QUAD,),
        in_specs=[COLS, COLS],
        out_specs=TILES,
        out_shape=TILES_SHAPE,
        cost_estimate=cost(0, 0, 64),
        compiler_params=PARAMS,
    )(a, b)


def merge_kernel(tiles_ref, a_ref, b_ref):
    for h in range(QUAD):
        a_ref[:, head(h)] = tiles_ref[h, 0]
        b_ref[:, head(h)] = tiles_ref[h, 1]


def merge_heads(tiles):
    return pl.pallas_call(
        merge_kernel,
        grid=(HEADS // QUAD,),
        in_specs=[TILES],
        out_specs=[COLS, COLS],
        out_shape=[ROWS_SHAPE, ROWS_SHAPE],
        cost_estimate=cost(0, 0, 64),
        compiler_params=PARAMS,
    )(tiles)


def local_stats_kernel(qd_ref, kv_ref, out_ref):
    for b in range(QUAD):
        q, d = qd_ref[b, 0], qd_ref[b, 1]
        near = (b, b ^ 1, b ^ 2)
        logits = [dot_last(kv_ref[c, 0], q) * INV_ROOT for c in near]
        top = max_rows(jnp.maximum(jnp.maximum(logits[0], logits[1]), logits[2]))
        exps = [jnp.exp(x - top) for x in logits]
        grads = [dot_last(kv_ref[c, 1], d) for c in near]
        out_ref[b, 0:1] = top
        out_ref[b, 1:2] = sum_rows(exps[0] + exps[1] + exps[2])
        out_ref[b, 2:3] = sum_rows(exps[0] * grads[0] + exps[1] * grads[1] + exps[2] * grads[2])
        out_ref[b, 3:8] = jnp.zeros((STAT_ROWS - 3, BLOCK), jnp.float32)


def local_stats(qd, kv):
    return pl.pallas_call(
        local_stats_kernel,
        grid=(HEADS // QUAD,),
        in_specs=[TILES, TILES],
        out_specs=STATS,
        out_shape=STATS_SHAPE,
        cost_estimate=cost(96, 48, 70),
        compiler_params=PARAMS,
    )(qd, kv)


def global_kernel(flags_ref, qd_ref, mine_ref, got_ref, stats_ref, sum_ref, out_ref):
    keys_mine = flags_ref[0] == 0
    key = jnp.where(keys_mine, mine_ref[...], got_ref[...])
    value = jnp.where(keys_mine, got_ref[...], mine_ref[...])
    key_sum = jnp.zeros((BLOCK, HEAD_DIM), jnp.float32)
    value_sum = jnp.zeros((BLOCK, HEAD_DIM), jnp.float32)
    for b in range(HEADS):
        q, d = qd_ref[b, 0], qd_ref[b, 1]
        logits = dot_last(key, q) * INV_ROOT
        grad = dot_last(value, d)
        local_top = stats_ref[b, 0:1]
        top = jnp.maximum(local_top, max_rows(logits))
        fade = jnp.exp(local_top - top)
        exps = jnp.exp(logits - top)
        scale = 1.0 / (stats_ref[b, 1:2] * fade + sum_rows(exps))
        delta = (stats_ref[b, 2:3] * fade + sum_rows(exps * grad)) * scale
        prob = exps * scale
        key_sum += dot((prob * (grad - delta)).astype(jnp.bfloat16), q)
        value_sum += dot(prob.astype(jnp.bfloat16), d)
        out_ref[b, 0:1] = top
        out_ref[b, 1:2] = scale
        out_ref[b, 2:3] = delta
        out_ref[b, 3:8] = jnp.zeros((STAT_ROWS - 3, BLOCK), jnp.float32)
    sum_ref[0] = key_sum * INV_ROOT
    sum_ref[1] = value_sum


def global_terms(flags, *arrays):
    return pl.pallas_call(
        global_kernel,
        in_specs=[SCALARS] + [WHOLE] * 4,
        out_specs=[WHOLE] * 2,
        out_shape=[PAIR_SHAPE, STATS_SHAPE],
        cost_estimate=cost(64, 16, 80),
        compiler_params=PARAMS,
    )(flags, *arrays)


def local_terms_kernel(flags_ref, qd_ref, kv_ref, stats_ref, out_ref, root_ref):
    step = pl.program_id(0)

    @pl.when(step == 0)
    def _():
        root_ref[...] = jnp.zeros_like(root_ref)

    for c in range(QUAD):
        k, v = kv_ref[c, 0], kv_ref[c, 1]
        key_sum = value_sum = None
        for a in (c, c ^ 1, c ^ 2):
            q, d = qd_ref[a, 0], qd_ref[a, 1]
            top, scale, delta = (stats_ref[a, i : i + 1] for i in range(3))
            prob = jnp.exp(dot_last(k, q) * INV_ROOT - top) * scale
            grad = dot_last(v, d)
            key_term = dot((prob * (grad - delta)).astype(jnp.bfloat16), q) * INV_ROOT
            value_term = dot(prob.astype(jnp.bfloat16), d)
            if a == c:
                key_sum, value_sum = key_term, value_term
            else:
                key_sum += key_term.astype(jnp.bfloat16).astype(jnp.float32)
                value_sum += value_term.astype(jnp.bfloat16).astype(jnp.float32)
        out_ref[c, 0] = key_sum.astype(jnp.bfloat16)
        out_ref[c, 1] = value_sum.astype(jnp.bfloat16)

        @pl.when(flags_ref[1] == step * QUAD + c)
        def _():
            root_ref[0] = key_sum
            root_ref[1] = value_sum


def local_terms(flags, *arrays):
    return pl.pallas_call(
        local_terms_kernel,
        grid=(HEADS // QUAD,),
        in_specs=[SCALARS, TILES, TILES, STATS],
        out_specs=[TILES, pl.BlockSpec((2, BLOCK, HEAD_DIM), lambda i: (0, 0, 0))],
        out_shape=[TILES_SHAPE, PAIR_SHAPE],
        cost_estimate=cost(192, 48, 100),
        compiler_params=PARAMS,
    )(flags, *arrays)


def body(queries, keys, values, dout, global_block):
    me = lax.axis_index("ctx")
    root = global_block[0]
    kind = (me >> PAIR_BIT) & 1
    keys_mine = kind == 0
    root_index = sum(((root >> bit) & 1) << i for i, bit in enumerate(TEAM))
    team_mask = sum(1 << bit for bit in TEAM)
    root_here = (root | team_mask) == (me | team_mask)
    flags = jnp.stack([kind, root_index]).astype(jnp.int32)

    kv = exchange(split_heads(keys, values), TEAM)
    qd, kv = lax.optimization_barrier((split_heads(queries, dout), kv))
    qd = exchange(qd, TEAM)

    held = lax.dynamic_index_in_dim(kv, root_index, 0, keepdims=False)
    got = swapped(jnp.where(keys_mine, held[1], held[0]), 1 << PAIR_BIT)
    root_kind = (root >> PAIR_BIT) & 1
    mine = jnp.where(root_kind == kind, jnp.where(keys_mine, held[0], held[1]), got)
    mine = picked(far_gather(mine), root, FAR)
    got = swapped(mine, 1 << PAIR_BIT)

    stats = local_stats(qd, kv)
    sums, stats = global_terms(flags, qd, mine, got, stats)

    send = jnp.where(keys_mine, sums[1], sums[0]).astype(jnp.bfloat16)
    part = jnp.where(keys_mine, sums[0], sums[1])
    part = part + swapped(send, 1 << PAIR_BIT).astype(jnp.float32)
    mine = added(far_gather(part.astype(jnp.bfloat16)))
    got = swapped(mine, 1 << PAIR_BIT)
    total = jnp.stack([jnp.where(keys_mine, mine, got), jnp.where(keys_mine, got, mine)])

    grads, root_grads = local_terms(flags, qd, kv, stats)
    root_grads = root_grads + jnp.where(root_here, total.astype(jnp.float32), 0.0)
    grads = lax.dynamic_update_index_in_dim(
        grads, root_grads.astype(jnp.bfloat16), root_index, 0
    )
    return tuple(merge_heads(exchange(grads, TEAM)))


def solution(mesh):
    rows = P(("dp", "ctx"), None)
    return jax.shard_map(
        body,
        mesh=mesh,
        in_specs=(rows, rows, rows, rows, P("dp")),
        out_specs=(rows, rows),
        check_vma=False,
    )
```

time: 269 us -> 212 us (0.79)
  the two profiles are of different devices: /device:TPU:66 before, /device:TPU:1 now
where the time goes in v2:
time: 212 us
  blocking collectives  98.2 us (46%)
  starting transfers between devices  44.8 us (21%)
  waiting for transfers between devices  42 us (20%)
  Pallas kernels  22.8 us (11%)
    all_gather x2, blocking collectives, far_gather(): return lax.all_gather(value, 'ctx', axis_index_groups=groups(FAR))  53.7 us
    all_to_all x1, blocking collectives, exchange(): return lax.all_to_all(value, 'ctx', 0, 0, axis_index_groups=groups(bits))  44.6 us
    all_to_all x2, waiting for transfers between devices, exchange(): return lax.all_to_all(value, 'ctx', 0, 0, axis_index_groups=groups(bits))  23.3 us
    ppermute x4, starting transfers between devices, swapped(): return lax.ppermute(value, 'ctx', pairs)  22.6 us
    all_to_all x2, starting transfers between devices, exchange(): return lax.all_to_all(value, 'ctx', 0, 0, axis_index_groups=groups(bits))  22.2 us
    ppermute x4, waiting for transfers between devices, swapped(): return lax.ppermute(value, 'ctx', pairs)  18.7 us
    pallas_call x1, Pallas kernels, local_terms(): pl.pallas_call(local_terms_kernel, grid=(HEADS // QUAD,), in_specs=[SCALA...  10.8 us
  transfers between devices with their start and end apart: 6, of which 3 were waited for; matrix products, arithmetic and copies ran while one was open for 0% of the time, Pallas kernels for 7%

profile of v2, /device:TPU:1, one launch (start us, length us, event | category | flops | bytes accessed | tf_op | source)
XLA Modules:
  0.0 211.6 jit_solution(18395819307932843137)
XLA Ops:
  0.6 0.0 copy-start
  0.6 1.0 copy-done
  1.7 0.0 copy-start.1
  1.7 1.0 copy-done.1
  2.7 1.7 shard_map.69
  4.4 0.0 copy-start.2
  4.4 0.0 copy-start.3
  4.4 17.7 %all-to-all-start = ((bf16[16,2,128,128]{3,2,1,0:T(8,128)(2,1)}), bf16[16,2,128,128]{3,2,1,0:T(8,128)(2,1)S(1)}, u32[]{:S(2)}, u32[]{:S(2)}) async-start(bf16[16,2,128,128]{3,2,1,0:T(8,128)(2,1)} %shard_map.69), calls=%async_computation | async-start | bytes 2097152 | tf_op jit(solution)/shard_map/all_to_all | solution.py:48
  22.1 0.0 copy-done.2
  22.2 0.0 copy-done.3
  22.2 1.7 shard_map.68
  23.9 23.3 %all-to-all-done.kv_ref = bf16[16,2,128,128]{3,2,1,0:T(8,128)(2,1)S(1)} async-done(((bf16[16,2,128,128]{3,2,1,0:T(8,128)(2,1)}), bf16[16,2,128,128]{3,2,1,0:T(8,128)(2,1)S(1)}, u32[]{:S(2)}, u32[]{:S(2)}) %all-to-all-start) | async-done | bytes 1048608 | tf_op jit(solution)/shard_map/all_to_all | solution.py:48
  47.2 4.4 %all-to-all-start.1 = ((bf16[16,2,128,128]{3,2,1,0:T(8,128)(2,1)}), bf16[16,2,128,128]{3,2,1,0:T(8,128)(2,1)S(1)}, u32[]{:S(2)}, u32[]{:S(2)}) async-start(bf16[16,2,128,128]{3,2,1,0:T(8,128)(2,1)} %shard_map.68), calls=%async_computation.1 | async-start | bytes 2097152 | tf_op jit(solution)/shard_map/all_to_all | solution.py:48
  52.3 1.9 collective-permute-start
  54.2 0.1 pad_add_fusion.flags_ref
  54.3 16.0 %collective-permute-done = bf16[128,128]{1,0:T(8,128)(2,1)S(1)} collective-permute-done((bf16[128,128]{1,0:T(8,128)(2,1)S(1)}, bf16[128,128]{1,0:T(8,128)(2,1)S(1)}, u32[]{:S(2)}, u32[]{:S(2)}) %collective-permute-start) | collective-permute-done | bytes 32800 | tf_op jit(solution)/shard_map/ppermute | solution.py:27
  70.3 29.4 %all-gather = bf16[512,128]{1,0:T(8,128)(2,1)S(1)} all-gather(bf16[128,128]{1,0:T(8,128)(2,1)S(1)} %bitcast_select_fusion), channel_id=2, replica_groups={{0,16,32,48},{1,17,33,49},{2,18,34,50},{3,19,35,51},{4,20,36,52},{5,21,..., dimensions={0}, use_global_device_ids=true | all-gather | bytes 163840 | tf_op jit(solution)/shard_map/all_gather | solution.py:52
  99.6 8.6 %collective-permute-start.1 = (bf16[128,128]{1,0:T(8,128)(2,1)S(1)}, bf16[128,128]{1,0:T(8,128)(2,1)S(1)}, u32[]{:S(2)}, u32[]{:S(2)}) collective-permute-start(bf16[128,128]{1,0:T(8,128)(2,1)S(1)} %dynamic-slice_bitcast_fusion.mine_ref), channel_id=1, source_target_pairs={{0,8},{1,9},{2,10},{3,11},{4,12},{5,13},{6,14},{7,15},{8,0},{9,1},... | collective-permute-start | bytes 98312 | tf_op jit(solution)/shard_map/ppermute | solution.py:27
  108.2 0.0 all-to-all-done.1.qd_ref
  108.2 2.8 %shard_map.70.stats_ref = f32[16,8,128]{2,1,0:T(8,128)S(1)} custom-call(bf16[16,2,128,128]{3,2,1,0:T(8,128)(2,1)S(1)} %all-to-all-done.1.qd_ref, bf16[16,2,128,128]{3,2,1,0:T(8,128)(2,1)S(1)} %all-to-all-done.kv_ref), custom_call_target="tpu_custom_call" | custom-call | flops 402653184 | bytes 2293760 | tf_op jit(solution)/shard_map/pallas_call | solution.py:153
  111.0 0.0 collective-permute-done.1.got_ref
  111.0 4.2 %shard_map.71 = (f32[2,128,128]{2,1,0:T(8,128)S(1)}, f32[16,8,128]{2,1,0:T(8,128)S(1)}) custom-call(s32[2]{0:T(128)S(1)} %pad_add_fusion.flags_ref, bf16[16,2,128,128]{3,2,1,0:T(8,128)(2,1)S(1)} %all-to-all-done.1.qd_ref, bf16[128,128]{1,0:T(8,128)(2,1)S(1)} %dynamic-slice_bitcast_fusion.mine_ref, bf16[128,128]{1,0:T(8,128)(2,1)S(1)} %collective-permute-done.1.got_ref, ...), custom_call_target="tpu_custom_call" | custom-call | flops 268435456 | bytes 2621440 | tf_op jit(solution)/shard_map/pallas_call | solution.py:192
  115.2 5.8 %collective-permute-start.2 = (bf16[128,128]{1,0:T(8,128)(2,1)S(1)}, bf16[128,128]{1,0:T(8,128)(2,1)S(1)}, u32[]{:S(2)}, u32[]{:S(2)}) collective-permute-start(bf16[128,128]{1,0:T(8,128)(2,1)S(1)} %fusion.3), channel_id=1, source_target_pairs={{0,8},{1,9},{2,10},{3,11},{4,12},{5,13},{6,14},{7,15},{8,0},{9,1},... | collective-permute-start | bytes 98312 | tf_op jit(solution)/shard_map/ppermute | solution.py:27
  121.1 2.7 %collective-permute-done.2 = bf16[128,128]{1,0:T(8,128)(2,1)S(1)} collective-permute-done((bf16[128,128]{1,0:T(8,128)(2,1)S(1)}, bf16[128,128]{1,0:T(8,128)(2,1)S(1)}, u32[]{:S(2)}, u32[]{:S(2)}) %collective-permute-start.2) | collective-permute-done | bytes 32800 | tf_op jit(solution)/shard_map/ppermute | solution.py:27
  123.8 24.3 %all-gather.1 = bf16[512,128]{1,0:T(8,128)(2,1)S(1)} all-gather(bf16[128,128]{1,0:T(8,128)(2,1)S(1)} %fusion.2), channel_id=3, replica_groups={{0,16,32,48},{1,17,33,49},{2,18,34,50},{3,19,35,51},{4,20,36,52},{5,21,..., dimensions={0}, use_global_device_ids=true | all-gather | bytes 163840 | tf_op jit(solution)/shard_map/all_gather | solution.py:52
  148.1 6.3 %collective-permute-start.3 = (bf16[128,128]{1,0:T(8,128)(2,1)S(1)}, bf16[128,128]{1,0:T(8,128)(2,1)S(1)}, u32[]{:S(2)}, u32[]{:S(2)}) collective-permute-start(bf16[128,128]{1,0:T(8,128)(2,1)S(1)} %add_convert_fusion.1), channel_id=1, source_target_pairs={{0,8},{1,9},{2,10},{3,11},{4,12},{5,13},{6,14},{7,15},{8,0},{9,1},... | collective-permute-start | bytes 98312 | tf_op jit(solution)/shard_map/ppermute | solution.py:27
  154.5 10.8 %shard_map.72 = (bf16[16,2,128,128]{3,2,1,0:T(8,128)(2,1)S(1)}, f32[2,128,128]{2,1,0:T(8,128)S(1)}) custom-call(s32[2]{0:T(128)S(1)} %pad_add_fusion.flags_ref, bf16[16,2,128,128]{3,2,1,0:T(8,128)(2,1)S(1)} %all-to-all-done.1.qd_ref, bf16[16,2,128,128]{3,2,1,0:T(8,128)(2,1)S(1)} %all-to-all-done.kv_ref, f32[16,8,128]{2,1,0:T(8,128)S(1)} %get-tuple-element.10.stats_ref), custom_call_target="tpu_custom_call" | custom-call | flops 805306368 | bytes 3276800 | tf_op jit(solution)/shard_map/pallas_call | solution.py:234
  165.4 0.0 collective-permute-done.3
  165.4 44.6 %all_to_all.15.tiles_ref = bf16[16,2,128,128]{3,2,1,0:T(8,128)(2,1)S(1)} all-to-all(bf16[16,2,128,128]{3,2,1,0:T(8,128)(2,1)S(1)} %fusion.1), channel_id=1, replica_groups={{0,1,2,3,4,5,6,7,64,65,66,67,68,69,70,71},{8,9,10,11,12,13,14,15,72,73,..., dimensions={0} | all-to-all | bytes 2097152 | tf_op jit(solution)/shard_map/all_to_all | solution.py:48
  210.0 1.6 shard_map.73
  (8 shorter events, 0.1 us)
Async XLA Ops:
  0.6 1.0 copy-start
  1.7 1.0 copy-start.1
  4.4 17.7 %copy-start.2 = (bf16[128,2048]{1,0:T(8,128)(2,1)S(1)}, bf16[128,2048]{1,0:T(8,128)(2,1)}, u32[]{:S(2)}) copy-start(bf16[128,2048]{1,0:T(8,128)(2,1)} %a_ref.2) | copy-start | bytes 1572868
  4.4 17.7 %copy-start.3 = (bf16[128,2048]{1,0:T(8,128)(2,1)S(1)}, bf16[128,2048]{1,0:T(8,128)(2,1)}, u32[]{:S(2)}) copy-start(bf16[128,2048]{1,0:T(8,128)(2,1)} %b_ref.2) | copy-start | bytes 1572868
  4.4 42.7 %all-to-all-start = ((bf16[16,2,128,128]{3,2,1,0:T(8,128)(2,1)}), bf16[16,2,128,128]{3,2,1,0:T(8,128)(2,1)S(1)}, u32[]{:S(2)}, u32[]{:S(2)}) async-start(bf16[16,2,128,128]{3,2,1,0:T(8,128)(2,1)} %shard_map.69), calls=%async_computation | async-start | bytes 2097152 | tf_op jit(solution)/shard_map/all_to_all | solution.py:48
  47.2 61.0 %all-to-all-start.1 = ((bf16[16,2,128,128]{3,2,1,0:T(8,128)(2,1)}), bf16[16,2,128,128]{3,2,1,0:T(8,128)(2,1)S(1)}, u32[]{:S(2)}, u32[]{:S(2)}) async-start(bf16[16,2,128,128]{3,2,1,0:T(8,128)(2,1)} %shard_map.68), calls=%async_computation.1 | async-start | bytes 2097152 | tf_op jit(solution)/shard_map/all_to_all | solution.py:48
  52.3 18.0 %collective-permute-start = (bf16[128,128]{1,0:T(8,128)(2,1)S(1)}, bf16[128,128]{1,0:T(8,128)(2,1)S(1)}, u32[]{:S(2)}, u32[]{:S(2)}) collective-permute-start(bf16[128,128]{1,0:T(8,128)(2,1)S(1)} %select_bitcast_fusion.2), channel_id=1, source_target_pairs={{0,8},{1,9},{2,10},{3,11},{4,12},{5,13},{6,14},{7,15},{8,0},{9,1},... | collective-permute-start | bytes 98312 | tf_op jit(solution)/shard_map/ppermute | solution.py:27
  99.6 11.4 %collective-permute-start.1 = (bf16[128,128]{1,0:T(8,128)(2,1)S(1)}, bf16[128,128]{1,0:T(8,128)(2,1)S(1)}, u32[]{:S(2)}, u32[]{:S(2)}) collective-permute-start(bf16[128,128]{1,0:T(8,128)(2,1)S(1)} %dynamic-slice_bitcast_fusion.mine_ref), channel_id=1, source_target_pairs={{0,8},{1,9},{2,10},{3,11},{4,12},{5,13},{6,14},{7,15},{8,0},{9,1},... | collective-permute-start | bytes 98312 | tf_op jit(solution)/shard_map/ppermute | solution.py:27
  115.2 8.6 %collective-permute-start.2 = (bf16[128,128]{1,0:T(8,128)(2,1)S(1)}, bf16[128,128]{1,0:T(8,128)(2,1)S(1)}, u32[]{:S(2)}, u32[]{:S(2)}) collective-permute-start(bf16[128,128]{1,0:T(8,128)(2,1)S(1)} %fusion.3), channel_id=1, source_target_pairs={{0,8},{1,9},{2,10},{3,11},{4,12},{5,13},{6,14},{7,15},{8,0},{9,1},... | collective-permute-start | bytes 98312 | tf_op jit(solution)/shard_map/ppermute | solution.py:27
  148.1 17.2 %collective-permute-start.3 = (bf16[128,128]{1,0:T(8,128)(2,1)S(1)}, bf16[128,128]{1,0:T(8,128)(2,1)S(1)}, u32[]{:S(2)}, u32[]{:S(2)}) collective-permute-start(bf16[128,128]{1,0:T(8,128)(2,1)S(1)} %add_convert_fusion.1), channel_id=1, source_target_pairs={{0,8},{1,9},{2,10},{3,11},{4,12},{5,13},{6,14},{7,15},{8,0},{9,1},... | collective-permute-start | bytes 98312 | tf_op jit(solution)/shard_map/ppermute | solution.py:27

commit v3 on v2

v3 whole, which is shorter than its diff:
```python
import functools

import jax
import jax.numpy as jnp
from jax import lax
from jax.experimental import pallas as pl
from jax.experimental.pallas import tpu as pltpu
from jax.sharding import PartitionSpec as P

HEADS = 16
HEAD_DIM = 128
BLOCK = 128
LEVELS = 2
WIDTH = HEADS * HEAD_DIM
INV_ROOT = HEAD_DIM ** (-0.5)
STEP_HEADS = 4
STEPS = HEADS // STEP_HEADS
STEP_COLS = STEP_HEADS * HEAD_DIM
STAT_ROWS = 8
TEAM = (0, 1, 6)
QUAD = 4
TEAM_SIZE = 8
TEAM_HEADS = 2
NEAR = (2, 3)
FAR = (4, 5)
LAST = (((1,), (1,)), ((), ()))


def groups(bits):
    spread = [
        sum(((k >> i) & 1) << bit for i, bit in enumerate(bits)) for k in range(1 << len(bits))
    ]
    mask = spread[-1]
    return [
        [base | part for part in spread]
        for base in range(lax.axis_size("ctx"))
        if not base & mask
    ]


def picked(root, bits):
    index = sum(((root >> bit) & 1) << i for i, bit in enumerate(bits))
    return index.astype(jnp.int32).reshape(1)


def exchange(value, bits):
    return lax.all_to_all(value, "ctx", 0, 0, axis_index_groups=groups(bits))


def sent(value, bits, source, target):
    spread_out = [
        sum(((k >> i) & 1) << bit for i, bit in enumerate(bits)) for k in range(1 << len(bits))
    ]
    pairs = [
        (base | spread_out[source], base | spread_out[target])
        for base in range(lax.axis_size("ctx"))
        if not base & spread_out[-1]
    ]
    return lax.ppermute(value, "ctx", pairs)


def by_root(root, bits, branch, *operands):
    branches = [functools.partial(branch, k) for k in range(1 << len(bits))]
    return lax.switch(picked(root, bits)[0], branches, *operands)


def dot_last(a, b):
    return lax.dot_general(a, b, LAST, preferred_element_type=jnp.float32)


def dot(a, b):
    return jnp.dot(a, b, preferred_element_type=jnp.float32)


def sum_rows(value):
    return jnp.sum(value, axis=0, keepdims=True)


def max_rows(value):
    return jnp.max(value, axis=0, keepdims=True)


def cost(dots, exps, size):
    return pl.CostEstimate(
        flops=2 * dots * BLOCK * BLOCK * HEAD_DIM,
        transcendentals=exps * BLOCK * BLOCK,
        bytes_accessed=size * BLOCK * HEAD_DIM * 2,
    )


PARAMS = pltpu.CompilerParams(vmem_limit_bytes=32 * 1024 * 1024)
FULL_PARAMS = pltpu.CompilerParams(vmem_limit_bytes=60 * 1024 * 1024)
SCALARS = pl.BlockSpec(memory_space=pltpu.SMEM)
COLS = pl.BlockSpec((BLOCK, QUAD * HEAD_DIM), lambda i: (0, i))
WHOLE = pl.BlockSpec(memory_space=pltpu.VMEM)
SQUARE = (BLOCK, HEAD_DIM)
LOW, FULL = jnp.bfloat16, jnp.float32
KINDS = 4
PARTS = 2 * TEAM_HEADS
STATS_SHAPE = (TEAM_HEADS, TEAM_SIZE, STAT_ROWS, BLOCK)


def shaped(shape, dtype):
    return jax.ShapeDtypeStruct(shape, dtype)


def head(h):
    return pl.ds(h * HEAD_DIM, HEAD_DIM)


def split_kernel(*refs):
    for kind, ref in enumerate(refs[:KINDS]):
        for h in range(QUAD):
            refs[-1][h, kind] = ref[:, head(h)]


def split_heads(*arrays):
    return pl.pallas_call(
        split_kernel,
        grid=(HEADS // QUAD,),
        in_specs=[COLS] * KINDS,
        out_specs=pl.BlockSpec((QUAD, KINDS) + SQUARE, lambda i: (i, 0, 0, 0)),
        out_shape=shaped((HEADS, KINDS) + SQUARE, LOW),
        cost_estimate=cost(0, 0, 128),
        compiler_params=FULL_PARAMS,
    )(*arrays)


def merge_kernel(tiles_ref, a_ref, b_ref):
    for h in range(QUAD):
        a_ref[:, head(h)] = tiles_ref[h, 0]
        b_ref[:, head(h)] = tiles_ref[h, 1]


def merge_heads(tiles):
    return pl.pallas_call(
        merge_kernel,
        grid=(HEADS // QUAD,),
        in_specs=[pl.BlockSpec((QUAD, 2) + SQUARE, lambda i: (i, 0, 0, 0))],
        out_specs=[COLS, COLS],
        out_shape=[shaped((BLOCK, WIDTH), LOW)] * 2,
        cost_estimate=cost(0, 0, 64),
        compiler_params=PARAMS,
    )(tiles)


def spread_kernel(index_ref, *refs):
    out_ref = refs[-1]
    for i, ref in enumerate(refs[:-1]):

        @pl.when(index_ref[0] == i)
        def _(ref=ref):
            for j in range(out_ref.shape[0]):
                out_ref[j] = ref[...]


def spread(copies, index, *arrays):
    return pl.pallas_call(
        spread_kernel,
        in_specs=[SCALARS] + [WHOLE] * len(arrays),
        out_specs=WHOLE,
        out_shape=shaped((copies,) + SQUARE, LOW),
        cost_estimate=cost(0, 0, 8),
        compiler_params=PARAMS,
    )(index, *arrays)


def added(arrays):
    a, b, c, d = (x.astype(FULL) for x in arrays)
    return ((a + b) + (c + d)).astype(LOW)


def local_stats_kernel(team_ref, out_ref):
    for b in range(QUAD):
        q, d = team_ref[b, 2], team_ref[b, 3]
        near = (b, b ^ 1, b ^ 2)
        logits = [dot_last(team_ref[c, 0], q) * INV_ROOT for c in near]
        top = max_rows(jnp.maximum(jnp.maximum(logits[0], logits[1]), logits[2]))
        exps = [jnp.exp(x - top) for x in logits]
        grads = [dot_last(team_ref[c, 1], d) for c in near]
        out_ref[0, b, 0:1] = top
        out_ref[0, b, 1:2] = sum_rows(exps[0] + exps[1] + exps[2])
        out_ref[0, b, 2:3] = sum_rows(exps[0] * grads[0] + exps[1] * grads[1] + exps[2] * grads[2])
        out_ref[0, b, 3:8] = jnp.zeros((STAT_ROWS - 3, BLOCK), jnp.float32)


def local_stats(team):
    return pl.pallas_call(
        local_stats_kernel,
        grid=(TEAM_SIZE // QUAD, TEAM_HEADS),
        in_specs=[pl.BlockSpec((QUAD, KINDS) + SQUARE, lambda i, j: (i, j, 0, 0))],
        out_specs=pl.BlockSpec((1, QUAD, STAT_ROWS, BLOCK), lambda i, j: (j, i, 0, 0)),
        out_shape=shaped(STATS_SHAPE, FULL),
        cost_estimate=cost(96, 48, 70),
        compiler_params=PARAMS,
    )(team)


def global_kernel(team_ref, kv_ref, stats_ref, sum_ref, out_ref):
    for j in range(TEAM_HEADS):
        key, value = kv_ref[2 * j], kv_ref[2 * j + 1]
        key_sum = jnp.zeros((BLOCK, HEAD_DIM), jnp.float32)
        value_sum = jnp.zeros((BLOCK, HEAD_DIM), jnp.float32)
        for b in range(TEAM_SIZE):
            q, d = team_ref[b, KINDS * j + 2], team_ref[b, KINDS * j + 3]
            logits = dot_last(key, q) * INV_ROOT
            grad = dot_last(value, d)
            local_top = stats_ref[j, b, 0:1]
            top = jnp.maximum(local_top, max_rows(logits))
            fade = jnp.exp(local_top - top)
            exps = jnp.exp(logits - top)
            scale = 1.0 / (stats_ref[j, b, 1:2] * fade + sum_rows(exps))
            delta = (stats_ref[j, b, 2:3] * fade + sum_rows(exps * grad)) * scale
            prob = exps * scale
            key_sum += dot((prob * (grad - delta)).astype(jnp.bfloat16), q)
            value_sum += dot(prob.astype(jnp.bfloat16), d)
            out_ref[j, b, 0:1] = top
            out_ref[j, b, 1:2] = scale
            out_ref[j, b, 2:3] = delta
            out_ref[j, b, 3:8] = jnp.zeros((STAT_ROWS - 3, BLOCK), jnp.float32)
        sum_ref[2 * j] = (key_sum * INV_ROOT).astype(sum_ref.dtype)
        sum_ref[2 * j + 1] = value_sum.astype(sum_ref.dtype)


def global_terms(*arrays):
    return pl.pallas_call(
        global_kernel,
        in_specs=[WHOLE] * 3,
        out_specs=[WHOLE] * 2,
        out_shape=[shaped((PARTS,) + SQUARE, LOW), shaped(STATS_SHAPE, FULL)],
        cost_estimate=cost(64, 16, 80),
        compiler_params=PARAMS,
    )(*arrays)


def local_terms_kernel(root_ref, team_ref, stats_ref, out_ref, sums_ref):
    quad = pl.program_id(1)
    for c in range(QUAD):
        k, v = team_ref[c, 0], team_ref[c, 1]
        key_sum = value_sum = None
        for a in (c, c ^ 1, c ^ 2):
            q, d = team_ref[a, 2], team_ref[a, 3]
            top, scale, delta = (stats_ref[0, a, i : i + 1] for i in range(3))
            prob = jnp.exp(dot_last(k, q) * INV_ROOT - top) * scale
            grad = dot_last(v, d)
            key_term = dot((prob * (grad - delta)).astype(jnp.bfloat16), q) * INV_ROOT
            value_term = dot(prob.astype(jnp.bfloat16), d)
            if a == c:
                key_sum, value_sum = key_term, value_term
            else:
                key_sum += key_term.astype(jnp.bfloat16).astype(jnp.float32)
                value_sum += value_term.astype(jnp.bfloat16).astype(jnp.float32)
        out_ref[c, 0] = key_sum.astype(jnp.bfloat16)
        out_ref[c, 1] = value_sum.astype(jnp.bfloat16)

        @pl.when(root_ref[0] == quad * QUAD + c)
        def _():
            sums_ref[0] = key_sum
            sums_ref[1] = value_sum


def local_terms(root_index, team, stats):
    return pl.pallas_call(
        local_terms_kernel,
        grid=(TEAM_HEADS, TEAM_SIZE // QUAD),
        in_specs=[
            SCALARS,
            pl.BlockSpec((QUAD, KINDS) + SQUARE, lambda j, i: (i, j, 0, 0)),
            pl.BlockSpec((1, QUAD, STAT_ROWS, BLOCK), lambda j, i: (j, i, 0, 0)),
        ],
        out_specs=[
            pl.BlockSpec((QUAD, 2) + SQUARE, lambda j, i: (i, j, 0, 0)),
            pl.BlockSpec((2,) + SQUARE, lambda j, i: (j, 0, 0)),
        ],
        out_shape=[shaped((TEAM_SIZE, PARTS) + SQUARE, LOW), shaped((PARTS,) + SQUARE, FULL)],
        cost_estimate=cost(192, 48, 100),
        compiler_params=PARAMS,
    )(root_index, team, stats)


def root_kernel(index_ref, here_ref, grads_ref, sums_ref, *refs):
    out_ref = refs[-1]
    for part, ref in enumerate(refs[:-1]):
        whole = (sums_ref[part] + ref[...].astype(FULL)).astype(LOW)
        out_ref[0, part] = jnp.where(here_ref[0] == 1, whole, grads_ref[0, part])


def add_root(index, here, grads, sums, *totals):
    block = pl.BlockSpec((1, PARTS) + SQUARE, lambda i, index_ref, here_ref: (index_ref[0], 0, 0, 0))
    whole = pl.BlockSpec((PARTS,) + SQUARE, lambda i, index_ref, here_ref: (0, 0, 0))
    square = pl.BlockSpec(SQUARE, lambda i, index_ref, here_ref: (0, 0))
    return pl.pallas_call(
        root_kernel,
        grid_spec=pltpu.PrefetchScalarGridSpec(
            num_scalar_prefetch=2,
            grid=(1,),
            in_specs=[block, whole] + [square] * len(totals),
            out_specs=block,
        ),
        out_shape=shaped(grads.shape, LOW),
        input_output_aliases={2: 0},
        cost_estimate=cost(0, 0, 28),
        compiler_params=PARAMS,
    )(index, here, grads, sums, *totals)


def body(queries, keys, values, dout, global_block):
    me = lax.axis_index("ctx")
    root = global_block[0]
    index = picked(root, TEAM)
    near, far = picked(me, NEAR), picked(me, FAR)
    team_mask = sum(1 << bit for bit in TEAM)
    here = ((root | team_mask) == (me | team_mask)).astype(jnp.int32).reshape(1)
    groups_near, groups_far = 1 << len(NEAR), 1 << len(FAR)

    def others(count, k):
        return [i for i in range(count) if i != k]

    def scatter_near(k, *parts):
        got = list(parts)
        for i in others(groups_near, k):
            got[i] = sent(parts[i], NEAR, k, i)
        return spread(1, near, *got)[0]

    def send_far(k, part):
        got = [part] * groups_far
        for i in others(groups_far, k):
            got[i] = sent(part, FAR, k, i)
        return spread(groups_near, far, *got)

    def sum_far(k, part, team, stats):
        got = [part] + [sent(part, FAR, i, k) for i in others(groups_far, k)]
        return (added(got),) + tuple(local_terms(index, team, stats))

    def gather_near(k, part):
        got = [part] * groups_near
        for i in others(groups_near, k):
            got[i] = sent(part, NEAR, i, k)
        return tuple(got)

    team = split_heads(keys, values, queries, dout)
    team = exchange(team.reshape((TEAM_SIZE, TEAM_HEADS * KINDS) + SQUARE), TEAM)

    held = lax.dynamic_index_in_dim(team, index[0], 0, keepdims=False)
    part = by_root(root, NEAR, scatter_near, *(held[i] for i in (0, 1, KINDS, KINDS + 1)))
    glob = exchange(by_root(root, FAR, send_far, part), NEAR)
    sums, stats = global_terms(team, glob, local_stats(team))

    part = added(exchange(sums, NEAR))
    part, grads, local_sums = by_root(root, FAR, sum_far, part, team, stats)
    totals = by_root(root, NEAR, gather_near, part)

    grads = exchange(add_root(index, here, grads, local_sums, *totals), TEAM)
    return tuple(merge_heads(grads.reshape((HEADS, 2) + SQUARE)))


def solution(mesh):
    rows = P(("dp", "ctx"), None)
    return jax.shard_map(
        body,
        mesh=mesh,
        in_specs=(rows, rows, rows, rows, P("dp")),
        out_specs=(rows, rows),
        check_vma=False,
    )
```

time: 212 us -> 166 us (0.78)
  the two profiles are of different devices: /device:TPU:1 before, /device:TPU:20 now
where the time goes in v3:
time: 166 us
  waiting for transfers between devices  81.9 us (49%)
  starting transfers between devices  39.5 us (24%)
  Pallas kernels  24.8 us (15%)
  blocking collectives  17.8 us (11%)
    all_to_all x3, waiting for transfers between devices, exchange(): return lax.all_to_all(value, 'ctx', 0, 0, axis_index_groups=groups(bits))  44.6 us
    ppermute x12, waiting for transfers between devices, sent(): return lax.ppermute(value, 'ctx', pairs)  37.3 us
    ppermute x12, starting transfers between devices, sent(): return lax.ppermute(value, 'ctx', pairs)  22.9 us
    all_to_all x1, blocking collectives, exchange(): return lax.all_to_all(value, 'ctx', 0, 0, axis_index_groups=groups(bits))  17.8 us
    all_to_all x3, starting transfers between devices, exchange(): return lax.all_to_all(value, 'ctx', 0, 0, axis_index_groups=groups(bits))  16.5 us
    pallas_call x1, Pallas kernels, local_terms(): pl.pallas_call(local_terms_kernel, grid=(TEAM_HEADS, TEAM_SIZE // QUAD),...  10.5 us
    pallas_call x1, Pallas kernels, global_terms(): pl.pallas_call(global_kernel, in_specs=[WHOLE] * 3, out_specs=[WHOLE] * 2...  4.17 us
    pallas_call x1, Pallas kernels, split_heads(): pl.pallas_call(split_kernel, grid=(HEADS // QUAD,), in_specs=[COLS] * KIN...  3.97 us
  transfers between devices with their start and end apart: 15, of which 6 were waited for; matrix products, arithmetic and copies ran while one was open for 0% of the time, Pallas kernels for 8%

profile of v3, /device:TPU:20, one launch (start us, length us, event | category | flops | bytes accessed | tf_op | source)
XLA Modules:
  0.0 165.5 jit_solution(14748813752108651789)
XLA Ops:
  0.6 4.0 %shard_map.68 = bf16[16,4,128,128]{3,2,1,0:T(8,128)(2,1)} custom-call(bf16[128,2048]{1,0:T(8,128)(2,1)} %refs_0_.1, bf16[128,2048]{1,0:T(8,128)(2,1)} %refs_1_.1, bf16[128,2048]{1,0:T(8,128)(2,1)} %refs_2_.1, bf16[128,2048]{1,0:T(8,128)(2,1)} %refs_3_.1), custom_call_target="tpu_custom_call" | custom-call | bytes 4194304 | tf_op jit(solution)/shard_map/pallas_call | solution.py:118
  4.6 3.9 %all-to-all-start = ((bf16[8,8,128,128]{3,2,1,0:T(8,128)(2,1)}), bf16[8,8,128,128]{3,2,1,0:T(8,128)(2,1)S(1)}, u32[]{:S(2)}, u32[]{:S(2)}) async-start(bf16[8,8,128,128]{3,2,1,0:T(8,128)(2,1)} %bitcast.30), calls=%async_computation | async-start | bytes 4194304 | tf_op jit(solution)/shard_map/all_to_all | solution.py:47
  9.2 26.0 %all-to-all-done.team_ref = bf16[8,8,128,128]{3,2,1,0:T(8,128)(2,1)S(1)} async-done(((bf16[8,8,128,128]{3,2,1,0:T(8,128)(2,1)}), bf16[8,8,128,128]{3,2,1,0:T(8,128)(2,1)S(1)}, u32[]{:S(2)}, u32[]{:S(2)}) %all-to-all-start) | async-done | bytes 2097184 | tf_op jit(solution)/shard_map/all_to_all | solution.py:47
  35.2 14.8 %conditional.4 = (bf16[128,128]{1,0:T(8,128)(2,1)S(1)}) conditional(s32[]{:T(128)} %bitcast.12, (bf16[128,128]{1,0:T(8,128)(2,1)S(1)}, bf16[128,128]{1,0:T(8,128)(2,1)S(1)}, bf16[128,128]{1,0:T(8,128)(2,1)S(1)}, s32[1]{0:T(128)}, bf16[128,128]{1,0:T(8,128)(2,1)S(1)}) %tuple.71, (bf16[128,128]{1,0:T(8,128)(2,1)S(1)}, ...), branch_computations={%region_0.1_spmd, %region_1.2_spmd, %region_2.3_spmd, %region_3.4_... | conditional | bytes 655488 | solution.py:64
  35.2 5.2 %collective-permute-start = (bf16[128,128]{1,0:T(8,128)(2,1)S(1)}, bf16[128,128]{1,0:T(8,128)(2,1)S(1)}, u32[]{:S(2)}, u32[]{:S(2)}) collective-permute-start(bf16[128,128]{1,0:T(8,128)(2,1)S(1)} %get-tuple-element.105), channel_id=1, source_target_pairs={{0,4},{1,5},{2,6},{3,7},{16,20},{17,21},{18,22},{19,23},{32,36},{3... | collective-permute-start | bytes 98312 | tf_op jit(solution)/shard_map/cond/branch_0_fun/ppermute | solution.py:59
  40.4 4.6 %collective-permute-start.1 = (bf16[128,128]{1,0:T(8,128)(2,1)S(1)}, bf16[128,128]{1,0:T(8,128)(2,1)S(1)}, u32[]{:S(2)}, u32[]{:S(2)}) collective-permute-start(bf16[128,128]{1,0:T(8,128)(2,1)S(1)} %get-tuple-element.106), channel_id=1, source_target_pairs={{0,8},{1,9},{2,10},{3,11},{16,24},{17,25},{18,26},{19,27},{32,40},... | collective-permute-start | bytes 98312 | tf_op jit(solution)/shard_map/cond/branch_0_fun/ppermute | solution.py:59
  45.0 3.4 %collective-permute-start.2 = (bf16[128,128]{1,0:T(8,128)(2,1)S(1)}, bf16[128,128]{1,0:T(8,128)(2,1)S(1)}, u32[]{:S(2)}, u32[]{:S(2)}) collective-permute-start(bf16[128,128]{1,0:T(8,128)(2,1)S(1)} %get-tuple-element.107), channel_id=1, source_target_pairs={{0,12},{1,13},{2,14},{3,15},{16,28},{17,29},{18,30},{19,31},{32,44... | collective-permute-start | bytes 98312 | tf_op jit(solution)/shard_map/cond/branch_0_fun/ppermute | solution.py:59
  48.3 0.0 collective-permute-done.refs_1_
  48.4 0.0 collective-permute-done.1.refs_2_
  48.4 1.6 collective-permute-done.2.refs_3_
  49.9 31.4 %conditional.5 = (bf16[4,128,128]{2,1,0:T(8,128)(2,1)}) conditional(s32[]{:T(128)} %bitcast.10, (bf16[128,128]{1,0:T(8,128)(2,1)S(1)}, s32[1]{0:T(128)}) %tuple.75, (bf16[128,128]{1,0:T(8,128)(2,1)S(1)}, s32[1]{0:T(128)}) %tuple.75, (bf16[128,128]{1,0:T(8,128)(2,1)S(1)}, s32[1]{0:T(128)}) %tuple.75, ...), branch_computations={%region_4.5_spmd, %region_5.6_spmd, %region_6.7_spmd, %region_7.8_... | conditional | bytes 655488 | solution.py:64
  49.9 0.7 collective-permute-start.20
  50.6 0.7 collective-permute-start.19
  51.3 1.3 collective-permute-start.18
  52.6 0.0 collective-permute-done.20.refs_3_
  52.6 0.0 collective-permute-done.19.refs_1_
  52.6 28.0 %collective-permute-done.18.refs_0_ = bf16[128,128]{1,0:T(8,128)(2,1)S(1)} collective-permute-done((bf16[128,128]{1,0:T(8,128)(2,1)S(1)}, bf16[128,128]{1,0:T(8,128)(2,1)S(1)}, u32[]{:S(2)}, u32[]{:S(2)}) %collective-permute-start.18) | collective-permute-done | bytes 32800 | tf_op jit(solution)/shard_map/cond/branch_2_fun/ppermute | solution.py:59
  80.6 0.7 branch_2_fun.4
  81.3 9.3 %all-to-all-start.1 = ((bf16[4,128,128]{2,1,0:T(8,128)(2,1)}), bf16[4,128,128]{2,1,0:T(8,128)(2,1)S(1)}, u32[]{:S(2)}, u32[]{:S(2)}) async-start(bf16[4,128,128]{2,1,0:T(8,128)(2,1)} %get-tuple-element.217), calls=%async_computation.1 | async-start | bytes 262144 | tf_op jit(solution)/shard_map/all_to_all | solution.py:47
  90.6 3.0 %shard_map.69.stats_ref = f32[2,8,8,128]{3,2,1,0:T(8,128)S(1)} custom-call(bf16[8,8,128,128]{3,2,1,0:T(8,128)(2,1)S(1)} %all-to-all-done.team_ref), custom_call_target="tpu_custom_call" | custom-call | flops 402653184 | bytes 2293760 | tf_op jit(solution)/shard_map/pallas_call | solution.py:188
  93.6 7.9 %all-to-all-done.1.kv_ref = bf16[4,128,128]{2,1,0:T(8,128)(2,1)S(1)} async-done(((bf16[4,128,128]{2,1,0:T(8,128)(2,1)}), bf16[4,128,128]{2,1,0:T(8,128)(2,1)S(1)}, u32[]{:S(2)}, u32[]{:S(2)}) %all-to-all-start.1) | async-done | bytes 131104 | tf_op jit(solution)/shard_map/all_to_all | solution.py:47
  101.4 4.2 %shard_map.70 = (bf16[4,128,128]{2,1,0:T(8,128)(2,1)}, f32[2,8,8,128]{3,2,1,0:T(8,128)S(1)}) custom-call(bf16[8,8,128,128]{3,2,1,0:T(8,128)(2,1)S(1)} %all-to-all-done.team_ref, bf16[4,128,128]{2,1,0:T(8,128)(2,1)S(1)} %all-to-all-done.1.kv_ref, f32[2,8,8,128]{3,2,1,0:T(8,128)S(1)} %shard_map.69.stats_ref), custom_call_target="tpu_custom_call" | custom-call | flops 268435456 | bytes 2621440 | tf_op jit(solution)/shard_map/pallas_call | solution.py:226
  105.6 3.3 %all-to-all-start.2 = ((bf16[4,128,128]{2,1,0:T(8,128)(2,1)}), bf16[4,128,128]{2,1,0:T(8,128)(2,1)S(1)}, u32[]{:S(2)}, u32[]{:S(2)}) async-start(bf16[4,128,128]{2,1,0:T(8,128)(2,1)} %get-tuple-element.167), calls=%async_computation.2 | async-start | bytes 262144 | tf_op jit(solution)/shard_map/all_to_all | solution.py:47
  109.0 10.7 %all-to-all-done.2 = bf16[4,128,128]{2,1,0:T(8,128)(2,1)S(1)} async-done(((bf16[4,128,128]{2,1,0:T(8,128)(2,1)}), bf16[4,128,128]{2,1,0:T(8,128)(2,1)S(1)}, u32[]{:S(2)}, u32[]{:S(2)}) %all-to-all-start.2) | async-done | bytes 131104 | tf_op jit(solution)/shard_map/all_to_all | solution.py:47
  119.7 14.0 %conditional.8 = (bf16[8,4,128,128]{3,2,1,0:T(8,128)(2,1)S(1)}, f32[4,128,128]{2,1,0:T(8,128)S(1)}, bf16[128,128]{1,0:T(8,128)(2,1)S(1)}) conditional(s32[]{:T(128)} %bitcast.10, (s32[1]{0:T(128)}, bf16[8,8,128,128]{3,2,1,0:T(8,128)(2,1)S(1)}, f32[2,8,8,128]{3,2,1,0:T(8,128)S(1)}, ...), branch_computations={%region_8.9_spmd, %region_9.10_spmd, %region_10.11_spmd, %region_1... | conditional | flops 805437440 | bytes 3834000
  119.7 0.7 collective-permute-start.43
  120.4 2.0 %collective-permute-start.42 = (bf16[128,128]{1,0:T(8,128)(2,1)S(1)}, bf16[128,128]{1,0:T(8,128)(2,1)S(1)}, u32[]{:S(2)}, u32[]{:S(2)}) collective-permute-start(bf16[128,128]{1,0:T(8,128)(2,1)S(1)} %bitcast.38), channel_id=1, source_target_pairs={{0,32},{1,33},{2,34},{3,35},{4,36},{5,37},{6,38},{7,39},{8,40},{9,... | collective-permute-start | bytes 98312 | tf_op jit(solution)/shard_map/cond/branch_2_fun/ppermute | solution.py:59
  122.4 0.7 collective-permute-start.44
  123.1 10.5 %branch_2_fun.5 = (bf16[8,4,128,128]{3,2,1,0:T(8,128)(2,1)S(1)}, f32[4,128,128]{2,1,0:T(8,128)S(1)}) custom-call(s32[1]{0:T(128)} %get-tuple-element.143.root_ref, bf16[8,8,128,128]{3,2,1,0:T(8,128)(2,1)S(1)} %get-tuple-element.144.team_ref, f32[2,8,8,128]{3,2,1,0:T(8,128)S(1)} %get-tuple-element.145.stats_ref), custom_call_target="tpu_custom_call" | custom-call | flops 805306368 | bytes 3276800 | tf_op jit(solution)/shard_map/cond/branch_2_fun/pallas_call | solution.py:263
  133.6 0.0 collective-permute-done.43
  133.6 0.0 collective-permute-done.42
  133.7 0.0 collective-permute-done.44
  133.7 11.6 %conditional.7 = (bf16[128,128]{1,0:T(8,128)(2,1)S(1)}, bf16[128,128]{1,0:T(8,128)(2,1)}, bf16[128,128]{1,0:T(8,128)(2,1)}, bf16[128,128]{1,0:T(8,128)(2,1)}) conditional(s32[]{:T(128)} %bitcast.12, bf16[128,128]{1,0:T(8,128)(2,1)S(1)} %get-tuple-element.179, bf16[128,128]{1,0:T(8,128)(2,1)S(1)} %get-tuple-element.179, ...), branch_computations={%region_12.13_spmd, %region_13.14_spmd, %region_14.15_spmd, %regio... | conditional | bytes 524440 | solution.py:64
  133.7 1.3 collective-permute-start.26
  135.0 1.3 collective-permute-start.25
  136.3 1.3 collective-permute-start.24
  137.6 7.7 %collective-permute-done.26 = bf16[128,128]{1,0:T(8,128)(2,1)} collective-permute-done((bf16[128,128]{1,0:T(8,128)(2,1)S(1)}, bf16[128,128]{1,0:T(8,128)(2,1)}, u32[]{:S(2)}, u32[]{:S(2)}) %collective-permute-start.26) | collective-permute-done | bytes 32800 | tf_op jit(solution)/shard_map/cond/branch_0_fun/ppermute | solution.py:59
  145.3 0.0 collective-permute-done.25
  145.3 0.0 collective-permute-done.24
  145.3 0.8 shard_map.71
  146.2 17.8 %all_to_all.20 = bf16[8,4,128,128]{3,2,1,0:T(8,128)(2,1)S(1)} all-to-all(bf16[8,4,128,128]{3,2,1,0:T(8,128)(2,1)S(1)} %shard_map.71), channel_id=1, replica_groups={{0,1,2,3,64,65,66,67},{4,5,6,7,68,69,70,71},{8,9,10,11,72,73,74,75},{12..., dimensions={0} | all-to-all | bytes 2097152 | tf_op jit(solution)/shard_map/all_to_all | solution.py:47
  164.0 1.6 shard_map.72
  (4 shorter events, 0.1 us)
Async XLA Ops:
  4.6 30.6 %all-to-all-start = ((bf16[8,8,128,128]{3,2,1,0:T(8,128)(2,1)}), bf16[8,8,128,128]{3,2,1,0:T(8,128)(2,1)S(1)}, u32[]{:S(2)}, u32[]{:S(2)}) async-start(bf16[8,8,128,128]{3,2,1,0:T(8,128)(2,1)} %bitcast.30), calls=%async_computation | async-start | bytes 4194304 | tf_op jit(solution)/shard_map/all_to_all | solution.py:47
  35.2 13.2 %collective-permute-start = (bf16[128,128]{1,0:T(8,128)(2,1)S(1)}, bf16[128,128]{1,0:T(8,128)(2,1)S(1)}, u32[]{:S(2)}, u32[]{:S(2)}) collective-permute-start(bf16[128,128]{1,0:T(8,128)(2,1)S(1)} %get-tuple-element.105), channel_id=1, source_target_pairs={{0,4},{1,5},{2,6},{3,7},{16,20},{17,21},{18,22},{19,23},{32,36},{3... | collective-permute-start | bytes 98312 | tf_op jit(solution)/shard_map/cond/branch_0_fun/ppermute | solution.py:59
  40.4 8.0 %collective-permute-start.1 = (bf16[128,128]{1,0:T(8,128)(2,1)S(1)}, bf16[128,128]{1,0:T(8,128)(2,1)S(1)}, u32[]{:S(2)}, u32[]{:S(2)}) collective-permute-start(bf16[128,128]{1,0:T(8,128)(2,1)S(1)} %get-tuple-element.106), channel_id=1, source_target_pairs={{0,8},{1,9},{2,10},{3,11},{16,24},{17,25},{18,26},{19,27},{32,40},... | collective-permute-start | bytes 98312 | tf_op jit(solution)/shard_map/cond/branch_0_fun/ppermute | solution.py:59
  45.0 5.0 %collective-permute-start.2 = (bf16[128,128]{1,0:T(8,128)(2,1)S(1)}, bf16[128,128]{1,0:T(8,128)(2,1)S(1)}, u32[]{:S(2)}, u32[]{:S(2)}) collective-permute-start(bf16[128,128]{1,0:T(8,128)(2,1)S(1)} %get-tuple-element.107), channel_id=1, source_target_pairs={{0,12},{1,13},{2,14},{3,15},{16,28},{17,29},{18,30},{19,31},{32,44... | collective-permute-start | bytes 98312 | tf_op jit(solution)/shard_map/cond/branch_0_fun/ppermute | solution.py:59
  49.9 2.6 %collective-permute-start.20 = (bf16[128,128]{1,0:T(8,128)(2,1)S(1)}, bf16[128,128]{1,0:T(8,128)(2,1)S(1)}, u32[]{:S(2)}, u32[]{:S(2)}) collective-permute-start(bf16[128,128]{1,0:T(8,128)(2,1)S(1)} %get-tuple-element.128.refs_2_), channel_id=1, source_target_pairs={{32,48},{33,49},{34,50},{35,51},{36,52},{37,53},{38,54},{39,55},{4... | collective-permute-start | bytes 98312 | tf_op jit(solution)/shard_map/cond/branch_2_fun/ppermute | solution.py:59
  50.6 2.0 %collective-permute-start.19 = (bf16[128,128]{1,0:T(8,128)(2,1)S(1)}, bf16[128,128]{1,0:T(8,128)(2,1)S(1)}, u32[]{:S(2)}, u32[]{:S(2)}) collective-permute-start(bf16[128,128]{1,0:T(8,128)(2,1)S(1)} %get-tuple-element.128.refs_2_), channel_id=1, source_target_pairs={{32,16},{33,17},{34,18},{35,19},{36,20},{37,21},{38,22},{39,23},{4... | collective-permute-start | bytes 98312 | tf_op jit(solution)/shard_map/cond/branch_2_fun/ppermute | solution.py:59
  51.3 29.3 %collective-permute-start.18 = (bf16[128,128]{1,0:T(8,128)(2,1)S(1)}, bf16[128,128]{1,0:T(8,128)(2,1)S(1)}, u32[]{:S(2)}, u32[]{:S(2)}) collective-permute-start(bf16[128,128]{1,0:T(8,128)(2,1)S(1)} %get-tuple-element.128.refs_2_), channel_id=1, source_target_pairs={{32,0},{33,1},{34,2},{35,3},{36,4},{37,5},{38,6},{39,7},{40,8},{41... | collective-permute-start | bytes 98312 | tf_op jit(solution)/shard_map/cond/branch_2_fun/ppermute | solution.py:59
  81.3 20.2 %all-to-all-start.1 = ((bf16[4,128,128]{2,1,0:T(8,128)(2,1)}), bf16[4,128,128]{2,1,0:T(8,128)(2,1)S(1)}, u32[]{:S(2)}, u32[]{:S(2)}) async-start(bf16[4,128,128]{2,1,0:T(8,128)(2,1)} %get-tuple-element.217), calls=%async_computation.1 | async-start | bytes 262144 | tf_op jit(solution)/shard_map/all_to_all | solution.py:47
  105.6 14.1 %all-to-all-start.2 = ((bf16[4,128,128]{2,1,0:T(8,128)(2,1)}), bf16[4,128,128]{2,1,0:T(8,128)(2,1)S(1)}, u32[]{:S(2)}, u32[]{:S(2)}) async-start(bf16[4,128,128]{2,1,0:T(8,128)(2,1)} %get-tuple-element.167), calls=%async_computation.2 | async-start | bytes 262144 | tf_op jit(solution)/shard_map/all_to_all | solution.py:47
  119.7 13.9 %collective-permute-start.43 = (bf16[128,128]{1,0:T(8,128)(2,1)S(1)}, bf16[128,128]{1,0:T(8,128)(2,1)S(1)}, u32[]{:S(2)}, u32[]{:S(2)}) collective-permute-start(bf16[128,128]{1,0:T(8,128)(2,1)S(1)} %bitcast.37), channel_id=1, source_target_pairs={{16,32},{17,33},{18,34},{19,35},{20,36},{21,37},{22,38},{23,39},{2... | collective-permute-start | bytes 98312 | tf_op jit(solution)/shard_map/cond/branch_2_fun/ppermute | solution.py:59
  120.4 13.2 %collective-permute-start.42 = (bf16[128,128]{1,0:T(8,128)(2,1)S(1)}, bf16[128,128]{1,0:T(8,128)(2,1)S(1)}, u32[]{:S(2)}, u32[]{:S(2)}) collective-permute-start(bf16[128,128]{1,0:T(8,128)(2,1)S(1)} %bitcast.38), channel_id=1, source_target_pairs={{0,32},{1,33},{2,34},{3,35},{4,36},{5,37},{6,38},{7,39},{8,40},{9,... | collective-permute-start | bytes 98312 | tf_op jit(solution)/shard_map/cond/branch_2_fun/ppermute | solution.py:59
  122.4 11.2 %collective-permute-start.44 = (bf16[128,128]{1,0:T(8,128)(2,1)S(1)}, bf16[128,128]{1,0:T(8,128)(2,1)S(1)}, u32[]{:S(2)}, u32[]{:S(2)}) collective-permute-start(bf16[128,128]{1,0:T(8,128)(2,1)S(1)} %bitcast.39), channel_id=1, source_target_pairs={{48,32},{49,33},{50,34},{51,35},{52,36},{53,37},{54,38},{55,39},{5... | collective-permute-start | bytes 98312 | tf_op jit(solution)/shard_map/cond/branch_2_fun/ppermute | solution.py:59
  133.7 11.6 %collective-permute-start.26 = (bf16[128,128]{1,0:T(8,128)(2,1)S(1)}, bf16[128,128]{1,0:T(8,128)(2,1)}, u32[]{:S(2)}, u32[]{:S(2)}) collective-permute-start(bf16[128,128]{1,0:T(8,128)(2,1)S(1)} %param.12), channel_id=1, source_target_pairs={{12,0},{13,1},{14,2},{15,3},{28,16},{29,17},{30,18},{31,19},{44,32... | collective-permute-start | bytes 98312 | tf_op jit(solution)/shard_map/cond/branch_0_fun/ppermute | solution.py:59
  135.0 10.3 %collective-permute-start.25 = (bf16[128,128]{1,0:T(8,128)(2,1)S(1)}, bf16[128,128]{1,0:T(8,128)(2,1)}, u32[]{:S(2)}, u32[]{:S(2)}) collective-permute-start(bf16[128,128]{1,0:T(8,128)(2,1)S(1)} %param.12), channel_id=1, source_target_pairs={{8,0},{9,1},{10,2},{11,3},{24,16},{25,17},{26,18},{27,19},{40,32},... | collective-permute-start | bytes 98312 | tf_op jit(solution)/shard_map/cond/branch_0_fun/ppermute | solution.py:59
  136.3 9.0 %collective-permute-start.24 = (bf16[128,128]{1,0:T(8,128)(2,1)S(1)}, bf16[128,128]{1,0:T(8,128)(2,1)}, u32[]{:S(2)}, u32[]{:S(2)}) collective-permute-start(bf16[128,128]{1,0:T(8,128)(2,1)S(1)} %param.12), channel_id=1, source_target_pairs={{4,0},{5,1},{6,2},{7,3},{20,16},{21,17},{22,18},{23,19},{36,32},{3... | collective-permute-start | bytes 98312 | tf_op jit(solution)/shard_map/cond/branch_0_fun/ppermute | solution.py:59
